TPU v7x, 32 devices: a whole 2x2x4 slice. The times are simulated.
32 devices in a mesh: flow: 8 (over z, x), cross: 4 (over y, core).
Axes of the slice: x: 2, y: 2, z: 4, core: 2. Of those that a mesh axis runs over, the one named last changes fastest.
Arguments:
- particles: float32 [1536, 8, 128], P(('flow', 'cross')), may hold values from -1.5 to 48, as said below
- counts: int32 [1536], P(('flow', 'cross')), may hold values from 32 to 128, as said below
- pairs: int32 [1536, 45], P(('flow', 'cross')), may hold values from 0 to 959, as said below
Outputs:
- rates: float32 [1536, 4, 128], P(('flow', 'cross'))
Inputs may be any that keep to these rules, and one draw needn't show every extreme that they name: `particles`: each block holds one cell of 1 x 2 x 2 (cells have y index in 0 to 7 and z index in 0 to 23); which cell a block holds follows one order, the same in every slab; positions lie inside their cell; density between 0.9 and 1.1, positive masses. `counts`: some block is full. `pairs`: the codes of a block name the blocks of its own cell and of its neighbour cells within one cell across (periodic) and two slabs along the flow.
All inputs are finite; a program needn't handle non-finite values.
Results may differ from a plain program's by a relative error of at most 0.0003.
Values sent between devices are 32-bit elements; how exact they have to be, the bound alone decides.
A program may use at most 64 MiB of HBM per device.

v0:
```python
import math

import jax
import jax.numpy as jnp
from jax import lax
from jax.sharding import PartitionSpec as P

GY = 8


kernel_coef = 5.0 * 21.0 / (16.0 * math.pi)
eta_square = 0.01
sound_speed = 6.0
delta_coef = 0.1
visc_coef = 0.1
group_blocks = 4
source_groups = 3


def passed_along(value, axis, steps):
    count = lax.axis_size(axis)
    pairs = [(source, (source + steps) % count) for source in range(count)]
    return lax.ppermute(value, axis, pairs)


def wrap_gap(gap, width):
    return gap - width * jnp.floor(gap / width + 0.5)


def partial_sums(target, sources, slab_gap, wide_y, wide_z):

    def target_field(field):
        return target[:, field][:, None, :, None]

    def source_field(field):
        return sources[:, :, field][:, :, None, :]

    gap_x = target_field(0) - source_field(0) - slab_gap[:, :, None, None]
    gap_y = wrap_gap(target_field(1) - source_field(1), wide_y)
    gap_z = wrap_gap(target_field(2) - source_field(2), wide_z)
    dist_sq = gap_x * gap_x + gap_y * gap_y + gap_z * gap_z
    radius = jnp.sqrt(dist_sq + eta_square)
    kernel = kernel_coef * jnp.maximum(1.0 - 0.5 * radius, 0.0) ** 3
    volume = (sources[:, :, 7] / sources[:, :, 6])[:, :, None, :]
    weight = volume * kernel
    rho_i = target_field(6)
    rho_j = source_field(6)
    closing = (
        (target_field(3) - source_field(3)) * gap_x
        + (target_field(4) - source_field(4)) * gap_y
        + (target_field(5) - source_field(5)) * gap_z
    )
    density_term = weight * (
        -rho_i * closing
        + 2.0 * delta_coef * sound_speed * (rho_j - rho_i) * dist_sq / (dist_sq + eta_square)
    )
    pressure_term = weight * (
        sound_speed * sound_speed * (rho_i - 1.0)
        + sound_speed * sound_speed * (rho_j - 1.0)
        - visc_coef * sound_speed * closing / (dist_sq + eta_square)
    )
    drho = jnp.sum(density_term, axis=(1, 3))
    sum_x = jnp.sum(pressure_term * gap_x, axis=(1, 3))
    sum_y = jnp.sum(pressure_term * gap_y, axis=(1, 3))
    sum_z = jnp.sum(pressure_term * gap_z, axis=(1, 3))
    return jnp.stack([drho, sum_x, sum_y, sum_z], axis=1)


def per_device(particles, counts, pairs):
    blocks = particles.shape[0]
    slots = particles.shape[2]
    slab_blk = blocks * lax.axis_size("cross")
    cells_z = slab_blk // GY
    slot_ids = jnp.arange(slots, dtype=jnp.int32)
    live = (slot_ids[None, :] < counts[:, None]).astype(jnp.float32)
    masked = jnp.concatenate([particles[:, :7], (particles[:, 7] * live)[:, None]], axis=1)
    nearby = {0: masked}
    for offset in (1, -1, 2, -2):
        nearby[offset] = passed_along(masked, "flow", -offset)
    slab_order = (-2, -1, 0, 1, 2)
    stacked = jnp.stack([nearby[offset] for offset in slab_order])
    stacked = lax.all_gather(stacked, "cross", axis=1, tiled=True)
    lookup = stacked.reshape((5 * slab_blk,) + particles.shape[1:])
    wide_y = 2.0 * GY
    wide_z = 2.0 * cells_z
    groups = blocks // group_blocks
    per_source = pairs.shape[1] // source_groups
    group_targets = particles.reshape(groups, group_blocks, particles.shape[1], slots)
    group_live = live.reshape(groups, group_blocks, slots)
    group_codes = pairs.reshape(groups, group_blocks, source_groups, per_source)

    def per_group(packed):
        target, target_live, codes = packed
        split_codes = jnp.transpose(codes, (1, 0, 2))

        def add_sources(total, code_part):
            sources = lookup[code_part]
            slab_gap = (code_part // slab_blk - 2).astype(jnp.float32)
            return (total + partial_sums(target, sources, slab_gap, wide_y, wide_z), None)

        start = jnp.zeros((group_blocks, 4, slots), jnp.float32)
        total, unused = lax.scan(add_sources, start, split_codes)
        accel = total[:, 1:] / target[:, 6][:, None, :]
        result = jnp.concatenate([total[:, :1], accel], axis=1)
        return result * target_live[:, None, :]

    output = lax.map(per_group, (group_targets, group_live, group_codes))
    return output.reshape(blocks, 4, slots)


def solution(mesh):
    placed = (P(("flow", "cross"), None, None), P(("flow", "cross")), P(("flow", "cross"), None))
    return jax.shard_map(
        per_device,
        mesh=mesh,
        in_specs=placed,
        out_specs=P(("flow", "cross"), None, None),
        check_vma=False,
    )
```

profile of v0, /device:TPU:2, one launch (start us, length us, event | category | flops | bytes accessed | tf_op | source)
XLA Modules:
  0.0 548.4 jit_solution(684843686075115995)
XLA Ops:
  14.5 3.9 collective-permute-done
  21.4 4.1 collective-permute-done.3
  28.2 31.9 %all-gather.2.cloned.1.call-done = f32[5,192,8,128]{3,2,1,0:T(8,128)} async-done(((f32[5,48,8,128]{3,2,1,0:T(8,128)}), f32[5,192,8,128]{3,2,1,0:T(8,128)}) %all-gather.2.cloned.1.call-update) | async-done | bytes 3932176 | tf_op jit(solution)/shard_map/all_gather | solution.py:82
  60.2 480.8 %while.36 = (s32[]{:T(128)}, f32[12,4,4,128]{3,2,1,0:T(4,128)S(1)}, s32[12,4,3,15]{3,1,2,0:T(4,128)S(1)}, f32[12,4,8,128]{3,2,1,0:T(8,128)}, f32[960,8,128]{2,1,...) while((s32[]{:T(128)}, f32[12,4,4,128]{3,2,1,0:T(4,128)S(1)}, ...), condition=%wide.region_7.8_spmd, body=%wide.region_0.7_spmd.sunk | while | flops 52149004 | bytes 2555700 | solution.py:107
  60.9 39.2 %while.37 = (s32[]{:T(128)}, f32[4,4,128]{2,0,1:T(4,128)S(1)}, f32[4,8,128]{2,0,1:T(4,128)S(1)}, s32[3,4,15]{2,1,0:T(4,128)S(1)}, f32[960,8,128]{2,1,0:T(8,128)}...) while((s32[]{:T(128)}, f32[4,4,128]{2,0,1:T(4,128)S(1)}, f32[4,8,128]{2,0,1:T(4,128)S(1)}, ...), condition=%wide.region_6.6_spmd.clone, body=%wide.region_1.5_spmd.clone.sunk | while | flops 52142860 | bytes 2425047 | solution.py:102
  61.0 2.7 gather_fusion
  64.2 9.8 %multiply_reduce_fusion.3 = (f32[4,128]{1,0:T(4,128)S(1)}, f32[4,128]{1,0:T(4,128)S(1)}, f32[4,128]{1,0:T(4,128)S(1)}, f32[4,128]{1,0:T(4,128)S(1)}) fusion(f32[4,15]{1,0:T(4,128)S(1)} %fusion.26, f32[4,15,128]{2,1,0:T(8,128)S(1)} %copy.112, f32[4,128]{1,0:T(4,128)S(1)} %get-tuple-element.419, f32[4,15,128]{2,1,0:T(8,128)S(1)} %copy.113, ...), kind=kLoop, calls=%fused_computation.25.clone.1 | loop fusion | flops 52099072 | bytes 303344 | tf_op jit(solution)/shard_map/while/body/eval_jaxpr/while/body/eval_jaxpr/reduce_sum | solution.py:63
  74.1 2.7 gather_fusion
  77.3 9.8 %multiply_reduce_fusion.3 = (f32[4,128]{1,0:T(4,128)S(1)}, f32[4,128]{1,0:T(4,128)S(1)}, f32[4,128]{1,0:T(4,128)S(1)}, f32[4,128]{1,0:T(4,128)S(1)}) fusion(f32[4,15]{1,0:T(4,128)S(1)} %fusion.26, f32[4,15,128]{2,1,0:T(8,128)S(1)} %copy.112, f32[4,128]{1,0:T(4,128)S(1)} %get-tuple-element.419, f32[4,15,128]{2,1,0:T(8,128)S(1)} %copy.113, ...), kind=kLoop, calls=%fused_computation.25.clone.1 | loop fusion | flops 52099072 | bytes 303344 | tf_op jit(solution)/shard_map/while/body/eval_jaxpr/while/body/eval_jaxpr/reduce_sum | solution.py:63
  87.2 2.7 gather_fusion
  90.3 9.8 %multiply_reduce_fusion.3 = (f32[4,128]{1,0:T(4,128)S(1)}, f32[4,128]{1,0:T(4,128)S(1)}, f32[4,128]{1,0:T(4,128)S(1)}, f32[4,128]{1,0:T(4,128)S(1)}) fusion(f32[4,15]{1,0:T(4,128)S(1)} %fusion.26, f32[4,15,128]{2,1,0:T(8,128)S(1)} %copy.112, f32[4,128]{1,0:T(4,128)S(1)} %get-tuple-element.419, f32[4,15,128]{2,1,0:T(8,128)S(1)} %copy.113, ...), kind=kLoop, calls=%fused_computation.25.clone.1 | loop fusion | flops 52099072 | bytes 303344 | tf_op jit(solution)/shard_map/while/body/eval_jaxpr/while/body/eval_jaxpr/reduce_sum | solution.py:63
  101.0 39.2 %while.37 = (s32[]{:T(128)}, f32[4,4,128]{2,0,1:T(4,128)S(1)}, f32[4,8,128]{2,0,1:T(4,128)S(1)}, s32[3,4,15]{2,1,0:T(4,128)S(1)}, f32[960,8,128]{2,1,0:T(8,128)}...) while((s32[]{:T(128)}, f32[4,4,128]{2,0,1:T(4,128)S(1)}, f32[4,8,128]{2,0,1:T(4,128)S(1)}, ...), condition=%wide.region_6.6_spmd.clone, body=%wide.region_1.5_spmd.clone.sunk | while | flops 52142860 | bytes 2425047 | solution.py:102
  104.3 9.8 %multiply_reduce_fusion.3 = (f32[4,128]{1,0:T(4,128)S(1)}, f32[4,128]{1,0:T(4,128)S(1)}, f32[4,128]{1,0:T(4,128)S(1)}, f32[4,128]{1,0:T(4,128)S(1)}) fusion(f32[4,15]{1,0:T(4,128)S(1)} %fusion.26, f32[4,15,128]{2,1,0:T(8,128)S(1)} %copy.112, f32[4,128]{1,0:T(4,128)S(1)} %get-tuple-element.419, f32[4,15,128]{2,1,0:T(8,128)S(1)} %copy.113, ...), kind=kLoop, calls=%fused_computation.25.clone.1 | loop fusion | flops 52099072 | bytes 303344 | tf_op jit(solution)/shard_map/while/body/eval_jaxpr/while/body/eval_jaxpr/reduce_sum | solution.py:63
  114.2 2.7 gather_fusion
  117.3 9.8 %multiply_reduce_fusion.3 = (f32[4,128]{1,0:T(4,128)S(1)}, f32[4,128]{1,0:T(4,128)S(1)}, f32[4,128]{1,0:T(4,128)S(1)}, f32[4,128]{1,0:T(4,128)S(1)}) fusion(f32[4,15]{1,0:T(4,128)S(1)} %fusion.26, f32[4,15,128]{2,1,0:T(8,128)S(1)} %copy.112, f32[4,128]{1,0:T(4,128)S(1)} %get-tuple-element.419, f32[4,15,128]{2,1,0:T(8,128)S(1)} %copy.113, ...), kind=kLoop, calls=%fused_computation.25.clone.1 | loop fusion | flops 52099072 | bytes 303344 | tf_op jit(solution)/shard_map/while/body/eval_jaxpr/while/body/eval_jaxpr/reduce_sum | solution.py:63
  127.2 2.7 gather_fusion
  130.4 9.8 %multiply_reduce_fusion.3 = (f32[4,128]{1,0:T(4,128)S(1)}, f32[4,128]{1,0:T(4,128)S(1)}, f32[4,128]{1,0:T(4,128)S(1)}, f32[4,128]{1,0:T(4,128)S(1)}) fusion(f32[4,15]{1,0:T(4,128)S(1)} %fusion.26, f32[4,15,128]{2,1,0:T(8,128)S(1)} %copy.112, f32[4,128]{1,0:T(4,128)S(1)} %get-tuple-element.419, f32[4,15,128]{2,1,0:T(8,128)S(1)} %copy.113, ...), kind=kLoop, calls=%fused_computation.25.clone.1 | loop fusion | flops 52099072 | bytes 303344 | tf_op jit(solution)/shard_map/while/body/eval_jaxpr/while/body/eval_jaxpr/reduce_sum | solution.py:63
  141.0 39.2 %while.37 = (s32[]{:T(128)}, f32[4,4,128]{2,0,1:T(4,128)S(1)}, f32[4,8,128]{2,0,1:T(4,128)S(1)}, s32[3,4,15]{2,1,0:T(4,128)S(1)}, f32[960,8,128]{2,1,0:T(8,128)}...) while((s32[]{:T(128)}, f32[4,4,128]{2,0,1:T(4,128)S(1)}, f32[4,8,128]{2,0,1:T(4,128)S(1)}, ...), condition=%wide.region_6.6_spmd.clone, body=%wide.region_1.5_spmd.clone.sunk | while | flops 52142860 | bytes 2425047 | solution.py:102
  141.2 2.7 gather_fusion
  144.3 9.8 %multiply_reduce_fusion.3 = (f32[4,128]{1,0:T(4,128)S(1)}, f32[4,128]{1,0:T(4,128)S(1)}, f32[4,128]{1,0:T(4,128)S(1)}, f32[4,128]{1,0:T(4,128)S(1)}) fusion(f32[4,15]{1,0:T(4,128)S(1)} %fusion.26, f32[4,15,128]{2,1,0:T(8,128)S(1)} %copy.112, f32[4,128]{1,0:T(4,128)S(1)} %get-tuple-element.419, f32[4,15,128]{2,1,0:T(8,128)S(1)} %copy.113, ...), kind=kLoop, calls=%fused_computation.25.clone.1 | loop fusion | flops 52099072 | bytes 303344 | tf_op jit(solution)/shard_map/while/body/eval_jaxpr/while/body/eval_jaxpr/reduce_sum | solution.py:63
  154.2 2.7 gather_fusion
  157.4 9.8 %multiply_reduce_fusion.3 = (f32[4,128]{1,0:T(4,128)S(1)}, f32[4,128]{1,0:T(4,128)S(1)}, f32[4,128]{1,0:T(4,128)S(1)}, f32[4,128]{1,0:T(4,128)S(1)}) fusion(f32[4,15]{1,0:T(4,128)S(1)} %fusion.26, f32[4,15,128]{2,1,0:T(8,128)S(1)} %copy.112, f32[4,128]{1,0:T(4,128)S(1)} %get-tuple-element.419, f32[4,15,128]{2,1,0:T(8,128)S(1)} %copy.113, ...), kind=kLoop, calls=%fused_computation.25.clone.1 | loop fusion | flops 52099072 | bytes 303344 | tf_op jit(solution)/shard_map/while/body/eval_jaxpr/while/body/eval_jaxpr/reduce_sum | solution.py:63
  167.3 2.7 gather_fusion
  170.5 9.8 %multiply_reduce_fusion.3 = (f32[4,128]{1,0:T(4,128)S(1)}, f32[4,128]{1,0:T(4,128)S(1)}, f32[4,128]{1,0:T(4,128)S(1)}, f32[4,128]{1,0:T(4,128)S(1)}) fusion(f32[4,15]{1,0:T(4,128)S(1)} %fusion.26, f32[4,15,128]{2,1,0:T(8,128)S(1)} %copy.112, f32[4,128]{1,0:T(4,128)S(1)} %get-tuple-element.419, f32[4,15,128]{2,1,0:T(8,128)S(1)} %copy.113, ...), kind=kLoop, calls=%fused_computation.25.clone.1 | loop fusion | flops 52099072 | bytes 303344 | tf_op jit(solution)/shard_map/while/body/eval_jaxpr/while/body/eval_jaxpr/reduce_sum | solution.py:63
  181.1 39.2 %while.37 = (s32[]{:T(128)}, f32[4,4,128]{2,0,1:T(4,128)S(1)}, f32[4,8,128]{2,0,1:T(4,128)S(1)}, s32[3,4,15]{2,1,0:T(4,128)S(1)}, f32[960,8,128]{2,1,0:T(8,128)}...) while((s32[]{:T(128)}, f32[4,4,128]{2,0,1:T(4,128)S(1)}, f32[4,8,128]{2,0,1:T(4,128)S(1)}, ...), condition=%wide.region_6.6_spmd.clone, body=%wide.region_1.5_spmd.clone.sunk | while | flops 52142860 | bytes 2425047 | solution.py:102
  181.2 2.7 gather_fusion
  184.4 9.8 %multiply_reduce_fusion.3 = (f32[4,128]{1,0:T(4,128)S(1)}, f32[4,128]{1,0:T(4,128)S(1)}, f32[4,128]{1,0:T(4,128)S(1)}, f32[4,128]{1,0:T(4,128)S(1)}) fusion(f32[4,15]{1,0:T(4,128)S(1)} %fusion.26, f32[4,15,128]{2,1,0:T(8,128)S(1)} %copy.112, f32[4,128]{1,0:T(4,128)S(1)} %get-tuple-element.419, f32[4,15,128]{2,1,0:T(8,128)S(1)} %copy.113, ...), kind=kLoop, calls=%fused_computation.25.clone.1 | loop fusion | flops 52099072 | bytes 303344 | tf_op jit(solution)/shard_map/while/body/eval_jaxpr/while/body/eval_jaxpr/reduce_sum | solution.py:63
  194.3 2.7 gather_fusion
  197.5 9.8 %multiply_reduce_fusion.3 = (f32[4,128]{1,0:T(4,128)S(1)}, f32[4,128]{1,0:T(4,128)S(1)}, f32[4,128]{1,0:T(4,128)S(1)}, f32[4,128]{1,0:T(4,128)S(1)}) fusion(f32[4,15]{1,0:T(4,128)S(1)} %fusion.26, f32[4,15,128]{2,1,0:T(8,128)S(1)} %copy.112, f32[4,128]{1,0:T(4,128)S(1)} %get-tuple-element.419, f32[4,15,128]{2,1,0:T(8,128)S(1)} %copy.113, ...), kind=kLoop, calls=%fused_computation.25.clone.1 | loop fusion | flops 52099072 | bytes 303344 | tf_op jit(solution)/shard_map/while/body/eval_jaxpr/while/body/eval_jaxpr/reduce_sum | solution.py:63
  210.5 9.8 %multiply_reduce_fusion.3 = (f32[4,128]{1,0:T(4,128)S(1)}, f32[4,128]{1,0:T(4,128)S(1)}, f32[4,128]{1,0:T(4,128)S(1)}, f32[4,128]{1,0:T(4,128)S(1)}) fusion(f32[4,15]{1,0:T(4,128)S(1)} %fusion.26, f32[4,15,128]{2,1,0:T(8,128)S(1)} %copy.112, f32[4,128]{1,0:T(4,128)S(1)} %get-tuple-element.419, f32[4,15,128]{2,1,0:T(8,128)S(1)} %copy.113, ...), kind=kLoop, calls=%fused_computation.25.clone.1 | loop fusion | flops 52099072 | bytes 303344 | tf_op jit(solution)/shard_map/while/body/eval_jaxpr/while/body/eval_jaxpr/reduce_sum | solution.py:63
  221.2 39.2 %while.37 = (s32[]{:T(128)}, f32[4,4,128]{2,0,1:T(4,128)S(1)}, f32[4,8,128]{2,0,1:T(4,128)S(1)}, s32[3,4,15]{2,1,0:T(4,128)S(1)}, f32[960,8,128]{2,1,0:T(8,128)}...) while((s32[]{:T(128)}, f32[4,4,128]{2,0,1:T(4,128)S(1)}, f32[4,8,128]{2,0,1:T(4,128)S(1)}, ...), condition=%wide.region_6.6_spmd.clone, body=%wide.region_1.5_spmd.clone.sunk | while | flops 52142860 | bytes 2425047 | solution.py:102
  221.3 2.7 gather_fusion
  224.5 9.8 %multiply_reduce_fusion.3 = (f32[4,128]{1,0:T(4,128)S(1)}, f32[4,128]{1,0:T(4,128)S(1)}, f32[4,128]{1,0:T(4,128)S(1)}, f32[4,128]{1,0:T(4,128)S(1)}) fusion(f32[4,15]{1,0:T(4,128)S(1)} %fusion.26, f32[4,15,128]{2,1,0:T(8,128)S(1)} %copy.112, f32[4,128]{1,0:T(4,128)S(1)} %get-tuple-element.419, f32[4,15,128]{2,1,0:T(8,128)S(1)} %copy.113, ...), kind=kLoop, calls=%fused_computation.25.clone.1 | loop fusion | flops 52099072 | bytes 303344 | tf_op jit(solution)/shard_map/while/body/eval_jaxpr/while/body/eval_jaxpr/reduce_sum | solution.py:63
  234.4 2.7 gather_fusion
  237.5 9.8 %multiply_reduce_fusion.3 = (f32[4,128]{1,0:T(4,128)S(1)}, f32[4,128]{1,0:T(4,128)S(1)}, f32[4,128]{1,0:T(4,128)S(1)}, f32[4,128]{1,0:T(4,128)S(1)}) fusion(f32[4,15]{1,0:T(4,128)S(1)} %fusion.26, f32[4,15,128]{2,1,0:T(8,128)S(1)} %copy.112, f32[4,128]{1,0:T(4,128)S(1)} %get-tuple-element.419, f32[4,15,128]{2,1,0:T(8,128)S(1)} %copy.113, ...), kind=kLoop, calls=%fused_computation.25.clone.1 | loop fusion | flops 52099072 | bytes 303344 | tf_op jit(solution)/shard_map/while/body/eval_jaxpr/while/body/eval_jaxpr/reduce_sum | solution.py:63
  250.6 9.8 %multiply_reduce_fusion.3 = (f32[4,128]{1,0:T(4,128)S(1)}, f32[4,128]{1,0:T(4,128)S(1)}, f32[4,128]{1,0:T(4,128)S(1)}, f32[4,128]{1,0:T(4,128)S(1)}) fusion(f32[4,15]{1,0:T(4,128)S(1)} %fusion.26, f32[4,15,128]{2,1,0:T(8,128)S(1)} %copy.112, f32[4,128]{1,0:T(4,128)S(1)} %get-tuple-element.419, f32[4,15,128]{2,1,0:T(8,128)S(1)} %copy.113, ...), kind=kLoop, calls=%fused_computation.25.clone.1 | loop fusion | flops 52099072 | bytes 303344 | tf_op jit(solution)/shard_map/while/body/eval_jaxpr/while/body/eval_jaxpr/reduce_sum | solution.py:63
  261.2 39.2 %while.37 = (s32[]{:T(128)}, f32[4,4,128]{2,0,1:T(4,128)S(1)}, f32[4,8,128]{2,0,1:T(4,128)S(1)}, s32[3,4,15]{2,1,0:T(4,128)S(1)}, f32[960,8,128]{2,1,0:T(8,128)}...) while((s32[]{:T(128)}, f32[4,4,128]{2,0,1:T(4,128)S(1)}, f32[4,8,128]{2,0,1:T(4,128)S(1)}, ...), condition=%wide.region_6.6_spmd.clone, body=%wide.region_1.5_spmd.clone.sunk | while | flops 52142860 | bytes 2425047 | solution.py:102
  264.5 9.8 %multiply_reduce_fusion.3 = (f32[4,128]{1,0:T(4,128)S(1)}, f32[4,128]{1,0:T(4,128)S(1)}, f32[4,128]{1,0:T(4,128)S(1)}, f32[4,128]{1,0:T(4,128)S(1)}) fusion(f32[4,15]{1,0:T(4,128)S(1)} %fusion.26, f32[4,15,128]{2,1,0:T(8,128)S(1)} %copy.112, f32[4,128]{1,0:T(4,128)S(1)} %get-tuple-element.419, f32[4,15,128]{2,1,0:T(8,128)S(1)} %copy.113, ...), kind=kLoop, calls=%fused_computation.25.clone.1 | loop fusion | flops 52099072 | bytes 303344 | tf_op jit(solution)/shard_map/while/body/eval_jaxpr/while/body/eval_jaxpr/reduce_sum | solution.py:63
  277.6 9.8 %multiply_reduce_fusion.3 = (f32[4,128]{1,0:T(4,128)S(1)}, f32[4,128]{1,0:T(4,128)S(1)}, f32[4,128]{1,0:T(4,128)S(1)}, f32[4,128]{1,0:T(4,128)S(1)}) fusion(f32[4,15]{1,0:T(4,128)S(1)} %fusion.26, f32[4,15,128]{2,1,0:T(8,128)S(1)} %copy.112, f32[4,128]{1,0:T(4,128)S(1)} %get-tuple-element.419, f32[4,15,128]{2,1,0:T(8,128)S(1)} %copy.113, ...), kind=kLoop, calls=%fused_computation.25.clone.1 | loop fusion | flops 52099072 | bytes 303344 | tf_op jit(solution)/shard_map/while/body/eval_jaxpr/while/body/eval_jaxpr/reduce_sum | solution.py:63
  290.7 9.8 %multiply_reduce_fusion.3 = (f32[4,128]{1,0:T(4,128)S(1)}, f32[4,128]{1,0:T(4,128)S(1)}, f32[4,128]{1,0:T(4,128)S(1)}, f32[4,128]{1,0:T(4,128)S(1)}) fusion(f32[4,15]{1,0:T(4,128)S(1)} %fusion.26, f32[4,15,128]{2,1,0:T(8,128)S(1)} %copy.112, f32[4,128]{1,0:T(4,128)S(1)} %get-tuple-element.419, f32[4,15,128]{2,1,0:T(8,128)S(1)} %copy.113, ...), kind=kLoop, calls=%fused_computation.25.clone.1 | loop fusion | flops 52099072 | bytes 303344 | tf_op jit(solution)/shard_map/while/body/eval_jaxpr/while/body/eval_jaxpr/reduce_sum | solution.py:63
  301.3 39.2 %while.37 = (s32[]{:T(128)}, f32[4,4,128]{2,0,1:T(4,128)S(1)}, f32[4,8,128]{2,0,1:T(4,128)S(1)}, s32[3,4,15]{2,1,0:T(4,128)S(1)}, f32[960,8,128]{2,1,0:T(8,128)}...) while((s32[]{:T(128)}, f32[4,4,128]{2,0,1:T(4,128)S(1)}, f32[4,8,128]{2,0,1:T(4,128)S(1)}, ...), condition=%wide.region_6.6_spmd.clone, body=%wide.region_1.5_spmd.clone.sunk | while | flops 52142860 | bytes 2425047 | solution.py:102
  304.6 9.8 %multiply_reduce_fusion.3 = (f32[4,128]{1,0:T(4,128)S(1)}, f32[4,128]{1,0:T(4,128)S(1)}, f32[4,128]{1,0:T(4,128)S(1)}, f32[4,128]{1,0:T(4,128)S(1)}) fusion(f32[4,15]{1,0:T(4,128)S(1)} %fusion.26, f32[4,15,128]{2,1,0:T(8,128)S(1)} %copy.112, f32[4,128]{1,0:T(4,128)S(1)} %get-tuple-element.419, f32[4,15,128]{2,1,0:T(8,128)S(1)} %copy.113, ...), kind=kLoop, calls=%fused_computation.25.clone.1 | loop fusion | flops 52099072 | bytes 303344 | tf_op jit(solution)/shard_map/while/body/eval_jaxpr/while/body/eval_jaxpr/reduce_sum | solution.py:63
  317.7 9.8 %multiply_reduce_fusion.3 = (f32[4,128]{1,0:T(4,128)S(1)}, f32[4,128]{1,0:T(4,128)S(1)}, f32[4,128]{1,0:T(4,128)S(1)}, f32[4,128]{1,0:T(4,128)S(1)}) fusion(f32[4,15]{1,0:T(4,128)S(1)} %fusion.26, f32[4,15,128]{2,1,0:T(8,128)S(1)} %copy.112, f32[4,128]{1,0:T(4,128)S(1)} %get-tuple-element.419, f32[4,15,128]{2,1,0:T(8,128)S(1)} %copy.113, ...), kind=kLoop, calls=%fused_computation.25.clone.1 | loop fusion | flops 52099072 | bytes 303344 | tf_op jit(solution)/shard_map/while/body/eval_jaxpr/while/body/eval_jaxpr/reduce_sum | solution.py:63
  330.7 9.8 %multiply_reduce_fusion.3 = (f32[4,128]{1,0:T(4,128)S(1)}, f32[4,128]{1,0:T(4,128)S(1)}, f32[4,128]{1,0:T(4,128)S(1)}, f32[4,128]{1,0:T(4,128)S(1)}) fusion(f32[4,15]{1,0:T(4,128)S(1)} %fusion.26, f32[4,15,128]{2,1,0:T(8,128)S(1)} %copy.112, f32[4,128]{1,0:T(4,128)S(1)} %get-tuple-element.419, f32[4,15,128]{2,1,0:T(8,128)S(1)} %copy.113, ...), kind=kLoop, calls=%fused_computation.25.clone.1 | loop fusion | flops 52099072 | bytes 303344 | tf_op jit(solution)/shard_map/while/body/eval_jaxpr/while/body/eval_jaxpr/reduce_sum | solution.py:63
  341.4 39.2 %while.37 = (s32[]{:T(128)}, f32[4,4,128]{2,0,1:T(4,128)S(1)}, f32[4,8,128]{2,0,1:T(4,128)S(1)}, s32[3,4,15]{2,1,0:T(4,128)S(1)}, f32[960,8,128]{2,1,0:T(8,128)}...) while((s32[]{:T(128)}, f32[4,4,128]{2,0,1:T(4,128)S(1)}, f32[4,8,128]{2,0,1:T(4,128)S(1)}, ...), condition=%wide.region_6.6_spmd.clone, body=%wide.region_1.5_spmd.clone.sunk | while | flops 52142860 | bytes 2425047 | solution.py:102
  344.7 9.8 %multiply_reduce_fusion.3 = (f32[4,128]{1,0:T(4,128)S(1)}, f32[4,128]{1,0:T(4,128)S(1)}, f32[4,128]{1,0:T(4,128)S(1)}, f32[4,128]{1,0:T(4,128)S(1)}) fusion(f32[4,15]{1,0:T(4,128)S(1)} %fusion.26, f32[4,15,128]{2,1,0:T(8,128)S(1)} %copy.112, f32[4,128]{1,0:T(4,128)S(1)} %get-tuple-element.419, f32[4,15,128]{2,1,0:T(8,128)S(1)} %copy.113, ...), kind=kLoop, calls=%fused_computation.25.clone.1 | loop fusion | flops 52099072 | bytes 303344 | tf_op jit(solution)/shard_map/while/body/eval_jaxpr/while/body/eval_jaxpr/reduce_sum | solution.py:63
  357.7 9.8 %multiply_reduce_fusion.3 = (f32[4,128]{1,0:T(4,128)S(1)}, f32[4,128]{1,0:T(4,128)S(1)}, f32[4,128]{1,0:T(4,128)S(1)}, f32[4,128]{1,0:T(4,128)S(1)}) fusion(f32[4,15]{1,0:T(4,128)S(1)} %fusion.26, f32[4,15,128]{2,1,0:T(8,128)S(1)} %copy.112, f32[4,128]{1,0:T(4,128)S(1)} %get-tuple-element.419, f32[4,15,128]{2,1,0:T(8,128)S(1)} %copy.113, ...), kind=kLoop, calls=%fused_computation.25.clone.1 | loop fusion | flops 52099072 | bytes 303344 | tf_op jit(solution)/shard_map/while/body/eval_jaxpr/while/body/eval_jaxpr/reduce_sum | solution.py:63
  370.8 9.8 %multiply_reduce_fusion.3 = (f32[4,128]{1,0:T(4,128)S(1)}, f32[4,128]{1,0:T(4,128)S(1)}, f32[4,128]{1,0:T(4,128)S(1)}, f32[4,128]{1,0:T(4,128)S(1)}) fusion(f32[4,15]{1,0:T(4,128)S(1)} %fusion.26, f32[4,15,128]{2,1,0:T(8,128)S(1)} %copy.112, f32[4,128]{1,0:T(4,128)S(1)} %get-tuple-element.419, f32[4,15,128]{2,1,0:T(8,128)S(1)} %copy.113, ...), kind=kLoop, calls=%fused_computation.25.clone.1 | loop fusion | flops 52099072 | bytes 303344 | tf_op jit(solution)/shard_map/while/body/eval_jaxpr/while/body/eval_jaxpr/reduce_sum | solution.py:63
  381.4 39.2 %while.37 = (s32[]{:T(128)}, f32[4,4,128]{2,0,1:T(4,128)S(1)}, f32[4,8,128]{2,0,1:T(4,128)S(1)}, s32[3,4,15]{2,1,0:T(4,128)S(1)}, f32[960,8,128]{2,1,0:T(8,128)}...) while((s32[]{:T(128)}, f32[4,4,128]{2,0,1:T(4,128)S(1)}, f32[4,8,128]{2,0,1:T(4,128)S(1)}, ...), condition=%wide.region_6.6_spmd.clone, body=%wide.region_1.5_spmd.clone.sunk | while | flops 52142860 | bytes 2425047 | solution.py:102
  384.7 9.8 %multiply_reduce_fusion.3 = (f32[4,128]{1,0:T(4,128)S(1)}, f32[4,128]{1,0:T(4,128)S(1)}, f32[4,128]{1,0:T(4,128)S(1)}, f32[4,128]{1,0:T(4,128)S(1)}) fusion(f32[4,15]{1,0:T(4,128)S(1)} %fusion.26, f32[4,15,128]{2,1,0:T(8,128)S(1)} %copy.112, f32[4,128]{1,0:T(4,128)S(1)} %get-tuple-element.419, f32[4,15,128]{2,1,0:T(8,128)S(1)} %copy.113, ...), kind=kLoop, calls=%fused_computation.25.clone.1 | loop fusion | flops 52099072 | bytes 303344 | tf_op jit(solution)/shard_map/while/body/eval_jaxpr/while/body/eval_jaxpr/reduce_sum | solution.py:63
  397.8 9.8 %multiply_reduce_fusion.3 = (f32[4,128]{1,0:T(4,128)S(1)}, f32[4,128]{1,0:T(4,128)S(1)}, f32[4,128]{1,0:T(4,128)S(1)}, f32[4,128]{1,0:T(4,128)S(1)}) fusion(f32[4,15]{1,0:T(4,128)S(1)} %fusion.26, f32[4,15,128]{2,1,0:T(8,128)S(1)} %copy.112, f32[4,128]{1,0:T(4,128)S(1)} %get-tuple-element.419, f32[4,15,128]{2,1,0:T(8,128)S(1)} %copy.113, ...), kind=kLoop, calls=%fused_computation.25.clone.1 | loop fusion | flops 52099072 | bytes 303344 | tf_op jit(solution)/shard_map/while/body/eval_jaxpr/while/body/eval_jaxpr/reduce_sum | solution.py:63
  410.9 9.8 %multiply_reduce_fusion.3 = (f32[4,128]{1,0:T(4,128)S(1)}, f32[4,128]{1,0:T(4,128)S(1)}, f32[4,128]{1,0:T(4,128)S(1)}, f32[4,128]{1,0:T(4,128)S(1)}) fusion(f32[4,15]{1,0:T(4,128)S(1)} %fusion.26, f32[4,15,128]{2,1,0:T(8,128)S(1)} %copy.112, f32[4,128]{1,0:T(4,128)S(1)} %get-tuple-element.419, f32[4,15,128]{2,1,0:T(8,128)S(1)} %copy.113, ...), kind=kLoop, calls=%fused_computation.25.clone.1 | loop fusion | flops 52099072 | bytes 303344 | tf_op jit(solution)/shard_map/while/body/eval_jaxpr/while/body/eval_jaxpr/reduce_sum | solution.py:63
  421.5 39.2 %while.37 = (s32[]{:T(128)}, f32[4,4,128]{2,0,1:T(4,128)S(1)}, f32[4,8,128]{2,0,1:T(4,128)S(1)}, s32[3,4,15]{2,1,0:T(4,128)S(1)}, f32[960,8,128]{2,1,0:T(8,128)}...) while((s32[]{:T(128)}, f32[4,4,128]{2,0,1:T(4,128)S(1)}, f32[4,8,128]{2,0,1:T(4,128)S(1)}, ...), condition=%wide.region_6.6_spmd.clone, body=%wide.region_1.5_spmd.clone.sunk | while | flops 52142860 | bytes 2425047 | solution.py:102
  424.8 9.8 %multiply_reduce_fusion.3 = (f32[4,128]{1,0:T(4,128)S(1)}, f32[4,128]{1,0:T(4,128)S(1)}, f32[4,128]{1,0:T(4,128)S(1)}, f32[4,128]{1,0:T(4,128)S(1)}) fusion(f32[4,15]{1,0:T(4,128)S(1)} %fusion.26, f32[4,15,128]{2,1,0:T(8,128)S(1)} %copy.112, f32[4,128]{1,0:T(4,128)S(1)} %get-tuple-element.419, f32[4,15,128]{2,1,0:T(8,128)S(1)} %copy.113, ...), kind=kLoop, calls=%fused_computation.25.clone.1 | loop fusion | flops 52099072 | bytes 303344 | tf_op jit(solution)/shard_map/while/body/eval_jaxpr/while/body/eval_jaxpr/reduce_sum | solution.py:63
  437.9 9.8 %multiply_reduce_fusion.3 = (f32[4,128]{1,0:T(4,128)S(1)}, f32[4,128]{1,0:T(4,128)S(1)}, f32[4,128]{1,0:T(4,128)S(1)}, f32[4,128]{1,0:T(4,128)S(1)}) fusion(f32[4,15]{1,0:T(4,128)S(1)} %fusion.26, f32[4,15,128]{2,1,0:T(8,128)S(1)} %copy.112, f32[4,128]{1,0:T(4,128)S(1)} %get-tuple-element.419, f32[4,15,128]{2,1,0:T(8,128)S(1)} %copy.113, ...), kind=kLoop, calls=%fused_computation.25.clone.1 | loop fusion | flops 52099072 | bytes 303344 | tf_op jit(solution)/shard_map/while/body/eval_jaxpr/while/body/eval_jaxpr/reduce_sum | solution.py:63
  450.9 9.8 %multiply_reduce_fusion.3 = (f32[4,128]{1,0:T(4,128)S(1)}, f32[4,128]{1,0:T(4,128)S(1)}, f32[4,128]{1,0:T(4,128)S(1)}, f32[4,128]{1,0:T(4,128)S(1)}) fusion(f32[4,15]{1,0:T(4,128)S(1)} %fusion.26, f32[4,15,128]{2,1,0:T(8,128)S(1)} %copy.112, f32[4,128]{1,0:T(4,128)S(1)} %get-tuple-element.419, f32[4,15,128]{2,1,0:T(8,128)S(1)} %copy.113, ...), kind=kLoop, calls=%fused_computation.25.clone.1 | loop fusion | flops 52099072 | bytes 303344 | tf_op jit(solution)/shard_map/while/body/eval_jaxpr/while/body/eval_jaxpr/reduce_sum | solution.py:63
  461.6 39.2 %while.37 = (s32[]{:T(128)}, f32[4,4,128]{2,0,1:T(4,128)S(1)}, f32[4,8,128]{2,0,1:T(4,128)S(1)}, s32[3,4,15]{2,1,0:T(4,128)S(1)}, f32[960,8,128]{2,1,0:T(8,128)}...) while((s32[]{:T(128)}, f32[4,4,128]{2,0,1:T(4,128)S(1)}, f32[4,8,128]{2,0,1:T(4,128)S(1)}, ...), condition=%wide.region_6.6_spmd.clone, body=%wide.region_1.5_spmd.clone.sunk | while | flops 52142860 | bytes 2425047 | solution.py:102
  464.9 9.8 %multiply_reduce_fusion.3 = (f32[4,128]{1,0:T(4,128)S(1)}, f32[4,128]{1,0:T(4,128)S(1)}, f32[4,128]{1,0:T(4,128)S(1)}, f32[4,128]{1,0:T(4,128)S(1)}) fusion(f32[4,15]{1,0:T(4,128)S(1)} %fusion.26, f32[4,15,128]{2,1,0:T(8,128)S(1)} %copy.112, f32[4,128]{1,0:T(4,128)S(1)} %get-tuple-element.419, f32[4,15,128]{2,1,0:T(8,128)S(1)} %copy.113, ...), kind=kLoop, calls=%fused_computation.25.clone.1 | loop fusion | flops 52099072 | bytes 303344 | tf_op jit(solution)/shard_map/while/body/eval_jaxpr/while/body/eval_jaxpr/reduce_sum | solution.py:63
  477.9 9.8 %multiply_reduce_fusion.3 = (f32[4,128]{1,0:T(4,128)S(1)}, f32[4,128]{1,0:T(4,128)S(1)}, f32[4,128]{1,0:T(4,128)S(1)}, f32[4,128]{1,0:T(4,128)S(1)}) fusion(f32[4,15]{1,0:T(4,128)S(1)} %fusion.26, f32[4,15,128]{2,1,0:T(8,128)S(1)} %copy.112, f32[4,128]{1,0:T(4,128)S(1)} %get-tuple-element.419, f32[4,15,128]{2,1,0:T(8,128)S(1)} %copy.113, ...), kind=kLoop, calls=%fused_computation.25.clone.1 | loop fusion | flops 52099072 | bytes 303344 | tf_op jit(solution)/shard_map/while/body/eval_jaxpr/while/body/eval_jaxpr/reduce_sum | solution.py:63
  491.0 9.8 %multiply_reduce_fusion.3 = (f32[4,128]{1,0:T(4,128)S(1)}, f32[4,128]{1,0:T(4,128)S(1)}, f32[4,128]{1,0:T(4,128)S(1)}, f32[4,128]{1,0:T(4,128)S(1)}) fusion(f32[4,15]{1,0:T(4,128)S(1)} %fusion.26, f32[4,15,128]{2,1,0:T(8,128)S(1)} %copy.112, f32[4,128]{1,0:T(4,128)S(1)} %get-tuple-element.419, f32[4,15,128]{2,1,0:T(8,128)S(1)} %copy.113, ...), kind=kLoop, calls=%fused_computation.25.clone.1 | loop fusion | flops 52099072 | bytes 303344 | tf_op jit(solution)/shard_map/while/body/eval_jaxpr/while/body/eval_jaxpr/reduce_sum | solution.py:63
  501.6 39.2 %while.37 = (s32[]{:T(128)}, f32[4,4,128]{2,0,1:T(4,128)S(1)}, f32[4,8,128]{2,0,1:T(4,128)S(1)}, s32[3,4,15]{2,1,0:T(4,128)S(1)}, f32[960,8,128]{2,1,0:T(8,128)}...) while((s32[]{:T(128)}, f32[4,4,128]{2,0,1:T(4,128)S(1)}, f32[4,8,128]{2,0,1:T(4,128)S(1)}, ...), condition=%wide.region_6.6_spmd.clone, body=%wide.region_1.5_spmd.clone.sunk | while | flops 52142860 | bytes 2425047 | solution.py:102
  504.9 9.8 %multiply_reduce_fusion.3 = (f32[4,128]{1,0:T(4,128)S(1)}, f32[4,128]{1,0:T(4,128)S(1)}, f32[4,128]{1,0:T(4,128)S(1)}, f32[4,128]{1,0:T(4,128)S(1)}) fusion(f32[4,15]{1,0:T(4,128)S(1)} %fusion.26, f32[4,15,128]{2,1,0:T(8,128)S(1)} %copy.112, f32[4,128]{1,0:T(4,128)S(1)} %get-tuple-element.419, f32[4,15,128]{2,1,0:T(8,128)S(1)} %copy.113, ...), kind=kLoop, calls=%fused_computation.25.clone.1 | loop fusion | flops 52099072 | bytes 303344 | tf_op jit(solution)/shard_map/while/body/eval_jaxpr/while/body/eval_jaxpr/reduce_sum | solution.py:63
  518.0 9.8 %multiply_reduce_fusion.3 = (f32[4,128]{1,0:T(4,128)S(1)}, f32[4,128]{1,0:T(4,128)S(1)}, f32[4,128]{1,0:T(4,128)S(1)}, f32[4,128]{1,0:T(4,128)S(1)}) fusion(f32[4,15]{1,0:T(4,128)S(1)} %fusion.26, f32[4,15,128]{2,1,0:T(8,128)S(1)} %copy.112, f32[4,128]{1,0:T(4,128)S(1)} %get-tuple-element.419, f32[4,15,128]{2,1,0:T(8,128)S(1)} %copy.113, ...), kind=kLoop, calls=%fused_computation.25.clone.1 | loop fusion | flops 52099072 | bytes 303344 | tf_op jit(solution)/shard_map/while/body/eval_jaxpr/while/body/eval_jaxpr/reduce_sum | solution.py:63
  531.1 9.8 %multiply_reduce_fusion.3 = (f32[4,128]{1,0:T(4,128)S(1)}, f32[4,128]{1,0:T(4,128)S(1)}, f32[4,128]{1,0:T(4,128)S(1)}, f32[4,128]{1,0:T(4,128)S(1)}) fusion(f32[4,15]{1,0:T(4,128)S(1)} %fusion.26, f32[4,15,128]{2,1,0:T(8,128)S(1)} %copy.112, f32[4,128]{1,0:T(4,128)S(1)} %get-tuple-element.419, f32[4,15,128]{2,1,0:T(8,128)S(1)} %copy.113, ...), kind=kLoop, calls=%fused_computation.25.clone.1 | loop fusion | flops 52099072 | bytes 303344 | tf_op jit(solution)/shard_map/while/body/eval_jaxpr/while/body/eval_jaxpr/reduce_sum | solution.py:63
  (924 shorter events, 104.4 us)
Async XLA Ops:
  6.5 53.6 %all-gather.2.cloned.1.call-start = ((), (), s32[]{:S(2)}) async-start(), calls=%async_computation | async-start | bytes 4915200 | tf_op jit(solution)/shard_map/all_gather | solution.py:82
  8.6 9.8 %collective-permute-start = (f32[48,8,128]{2,1,0:T(8,128)S(1)}, f32[48,8,128]{2,1,0:T(8,128)S(1)}, u32[]{:S(2)}, u32[]{:S(2)}) collective-permute-start(f32[48,8,128]{2,1,0:T(8,128)S(1)} %pad_maximum_fusion), channel_id=1, source_target_pairs={{0,8},{4,12},{8,16},{12,20},{16,24},{20,28},{24,0},{28,4},{1,9},{5... | collective-permute-start | bytes 589832 | tf_op jit(solution)/shard_map/ppermute | solution.py:23
  10.2 9.6 %collective-permute-start.1 = (f32[48,8,128]{2,1,0:T(8,128)S(1)}, f32[48,8,128]{2,1,0:T(8,128)S(1)}, u32[]{:S(2)}, u32[]{:S(2)}) collective-permute-start(f32[48,8,128]{2,1,0:T(8,128)S(1)} %pad_maximum_fusion), channel_id=1, source_target_pairs={{0,4},{4,8},{8,12},{12,16},{16,20},{20,24},{24,28},{28,0},{1,5},{5... | collective-permute-start | bytes 589832 | tf_op jit(solution)/shard_map/ppermute | solution.py:23
  11.7 9.7 %collective-permute-start.2 = (f32[48,8,128]{2,1,0:T(8,128)S(1)}, f32[48,8,128]{2,1,0:T(8,128)S(1)}, u32[]{:S(2)}, u32[]{:S(2)}) collective-permute-start(f32[48,8,128]{2,1,0:T(8,128)S(1)} %pad_maximum_fusion), channel_id=1, source_target_pairs={{0,28},{4,0},{8,4},{12,8},{16,12},{20,16},{24,20},{28,24},{1,29},{... | collective-permute-start | bytes 589832 | tf_op jit(solution)/shard_map/ppermute | solution.py:23
  12.2 13.3 %collective-permute-start.3 = (f32[48,8,128]{2,1,0:T(8,128)S(1)}, f32[48,8,128]{2,1,0:T(8,128)S(1)}, u32[]{:S(2)}, u32[]{:S(2)}) collective-permute-start(f32[48,8,128]{2,1,0:T(8,128)S(1)} %pad_maximum_fusion), channel_id=1, source_target_pairs={{0,24},{4,28},{8,0},{12,4},{16,8},{20,12},{24,16},{28,20},{1,25},{... | collective-permute-start | bytes 589832 | tf_op jit(solution)/shard_map/ppermute | solution.py:23
  25.6 0.9 copy-start
  540.9 0.6 copy-start.1
Sparse Core Ops, SparseCore 0:
  26.7 33.4 all-gather.1
where the time goes:
time: 552 us; the launch traced here: 548 us
  other arithmetic  357 us (65%)
  local copies, waits for them, and re-layouts  122 us (22%)
  waiting for transfers between devices  42 us (8%)
  between operations  13.5 us (2%)
  loops' own time  7.16 us (1%)
  starting transfers between devices  5.9 us (1%)
    reduce_sum x36, other arithmetic, partial_sums(): sum_x = jnp.sum(pressure_term * gap_x, axis=(1, 3))  351 us
    gather x36, local copies, waits for them, and re-layouts, add_sources(): sources = lookup[code_part]  97.3 us
    all_gather x1, waiting for transfers between devices, per_device(): stacked = lax.all_gather(stacked, 'cross', axis=1, tiled=True)  31.9 us
  transfers between devices with their start and end apart: 5, of which 5 were waited for; matrix products, arithmetic and copies ran while one was open for 0% of the time, Pallas kernels for 0%

commit v1 on v0

v1 whole, which is shorter than its diff:
```python
import functools
import math

import jax
import jax.numpy as jnp
from jax import lax
from jax.experimental import pallas as pl
from jax.experimental.pallas import tpu as pltpu
from jax.sharding import PartitionSpec as P

GY = 8


kernel_coef = 5.0 * 21.0 / (16.0 * math.pi)
eta_square = 0.01
sound_speed = 6.0
delta_coef = 0.1
visc_coef = 0.1
slab_order = (-2, -1, 0, 1, 2)
wave = sound_speed * visc_coef
stiff = sound_speed / visc_coef
rows_step = 16
fields = 7


def passed_along(value, axis, steps):
    count = lax.axis_size(axis)
    pairs = [(source, (source + steps) % count) for source in range(count)]
    return lax.ppermute(value, axis, pairs)


def pair_kernel(per_block, wide_y, wide_z, codes, live_counts, source_counts, target, columns, lookup, out, packed, spread, totals):
    block = pl.program_id(0)
    slots = target.shape[2]
    lanes = lax.broadcasted_iota(jnp.int32, (8, slots), 1)
    row = lax.broadcasted_iota(jnp.int32, (8, slots), 0)
    wide = jnp.where(row == 1, wide_y, jnp.where(row == 2, wide_z, 0.0))
    inverse = jnp.where(row == 1, 1.0 / wide_y, jnp.where(row == 2, 1.0 / wide_z, 0.0))
    own = target[0]
    own_first = jnp.broadcast_to(own[:, 0:1], (8, slots)) * inverse + 0.5

    def pack(step, state):
        current, tile, start = state
        code = codes[block * per_block + step]
        count = source_counts[code]
        value = lookup[code]
        first = jnp.broadcast_to(value[:, 0:1], (8, slots))
        value = value + wide * jnp.floor(own_first - first * inverse)
        turned = pltpu.roll(value, start, 1)
        ahead = lanes >= start
        merged = jnp.where(ahead, turned, current)
        packed[tile] = merged
        end = start + count
        full = (end >= slots).astype(jnp.int32)
        keep = jnp.broadcast_to(full, (8, slots)) == 0
        rest = jnp.where(ahead, 0.0, turned)
        return jnp.where(keep, merged, rest), tile + full, end - full * slots

    empty = jnp.zeros((8, slots), jnp.float32)
    current, tile, start = lax.fori_loop(0, per_block, pack, (empty, jnp.int32(0), jnp.int32(0)), unroll=5)
    packed[tile] = current
    packed[tile + 1] = empty
    tiles = tile + (start > 0).astype(jnp.int32)

    for group in range(slots // 8):
        part = columns[0, group * 8:group * 8 + 8, :]
        for field in range(fields):
            spread[field, group * 8:group * 8 + 8, :] = jnp.broadcast_to(part[:, field:field + 1], (8, slots))

    live = live_counts[block]

    def per_rows(index, unused):
        first = pl.multiple_of(index * rows_step, rows_step)
        rows = pl.ds(first, rows_step)
        xi, yi, zi, ui, vi, wi, pi = [spread[field, rows, :] for field in range(fields)]

        def one_tile(place, sums):
            s_close, s_diff, s_damp, s_x, s_y, s_z = sums
            xj, yj, zj, uj, vj, wj, pj, volume = [packed[place, field:field + 1, :] for field in range(8)]
            gap_x = xi - xj
            gap_y = yi - yj
            gap_z = zi - zj
            shifted = (gap_x * gap_x + eta_square) + (gap_y * gap_y + gap_z * gap_z)
            inv = lax.rsqrt(shifted)
            bump = jnp.maximum(2.0 - shifted * inv, 0.0)
            weight = (bump * bump) * (bump * volume)
            closing = (ui - uj) * gap_x + (vi - vj) * gap_y + (wi - wj) * gap_z
            inv_sq = inv * inv
            diff = weight * (pj - pi)
            push = weight * ((pi + pj) - closing * inv_sq)
            return (
                s_close + weight * closing,
                s_diff + diff,
                s_damp + diff * inv_sq,
                s_x + push * gap_x,
                s_y + push * gap_y,
                s_z + push * gap_z,
            )

        def two_tiles(place, sums):
            return one_tile(2 * place + 1, one_tile(2 * place, sums))

        zero = jnp.zeros((rows_step, slots), jnp.float32)
        sums = lax.fori_loop(0, (tiles + 1) // 2, two_tiles, (zero,) * 6)
        totals[0, rows, :] = sums[0]
        totals[1, rows, :] = sums[1] - eta_square * sums[2]
        totals[2, rows, :] = sums[3]
        totals[3, rows, :] = sums[4]
        totals[4, rows, :] = sums[5]
        return unused

    lax.fori_loop(0, (live + rows_step - 1) // rows_step, per_rows, 0)

    ones = jnp.ones((8, slots), jnp.float32)

    def summed(which):
        return lax.dot_general(
            ones, totals[which], (((1,), (1,)), ((), ())),
            precision=lax.Precision.HIGHEST, preferred_element_type=jnp.float32,
        )[0:1]

    rho = own[6:7]
    scale = kernel_coef / 8.0
    drho = scale * (2.0 * delta_coef * sound_speed / stiff * summed(1) - rho * summed(0))
    over = (scale * wave) / rho
    alive = lanes[0:1] < live
    out[0, 0:1, :] = jnp.where(alive, drho, 0.0)
    for axis in range(3):
        out[0, axis + 1:axis + 2, :] = jnp.where(alive, over * summed(2 + axis), 0.0)


def per_device(particles, counts, pairs):
    blocks, width, slots = particles.shape
    slab_blk = blocks * lax.axis_size("cross")
    cells_z = slab_blk // GY
    per_block = pairs.shape[1]
    slot_ids = jnp.arange(slots, dtype=jnp.int32)
    live = (slot_ids[None, :] < counts[:, None]).astype(jnp.float32)
    rho = particles[:, 6]
    pressure = stiff * (rho - 1.0)
    volume = particles[:, 7] / rho * live
    ready = jnp.concatenate([particles[:, :6], pressure[:, None], volume[:, None]], axis=1)
    nearby = {0: ready}
    for offset in (1, -1, 2, -2):
        nearby[offset] = passed_along(ready, "flow", -offset)
    along = (jnp.arange(width) == 0).astype(jnp.float32)[:, None]
    stacked = jnp.stack([nearby[offset] + offset * along for offset in slab_order])
    stacked = lax.all_gather(stacked, "cross", axis=1, tiled=True)
    lookup = stacked.reshape((5 * slab_blk, width, slots))
    source_counts = jnp.max(jnp.where(lookup[:, 7] > 0.0, slot_ids[None, :] + 1, 0), axis=1)
    columns = jnp.swapaxes(ready, 1, 2)
    body = functools.partial(pair_kernel, per_block, 2.0 * GY, 2.0 * cells_z)
    return pl.pallas_call(
        body,
        out_shape=jax.ShapeDtypeStruct((blocks, 4, slots), jnp.float32),
        grid_spec=pltpu.PrefetchScalarGridSpec(
            num_scalar_prefetch=3,
            grid=(blocks,),
            in_specs=[
                pl.BlockSpec((1, width, slots), lambda i, *_: (i, 0, 0)),
                pl.BlockSpec((1, slots, width), lambda i, *_: (i, 0, 0)),
                pl.BlockSpec(memory_space=pltpu.VMEM),
            ],
            out_specs=pl.BlockSpec((1, 4, slots), lambda i, *_: (i, 0, 0)),
            scratch_shapes=[
                pltpu.VMEM((per_block + 2, 8, slots), jnp.float32),
                pltpu.VMEM((fields, slots, slots), jnp.float32),
                pltpu.VMEM((5, slots, slots), jnp.float32),
            ],
        ),
        compiler_params=pltpu.CompilerParams(vmem_limit_bytes=40 * 1024 * 1024),
        name="pair_rates",
    )(pairs.reshape(-1), counts, source_counts, particles, columns, lookup)


def solution(mesh):
    placed = (P(("flow", "cross"), None, None), P(("flow", "cross")), P(("flow", "cross"), None))
    return jax.shard_map(
        per_device,
        mesh=mesh,
        in_specs=placed,
        out_specs=P(("flow", "cross"), None, None),
        check_vma=False,
    )
```

time: 552 us -> 333 us (0.60)
  other arithmetic: 357 us -> 24.2 us
  Pallas kernels: 0 us -> 232 us
  local copies, waits for them, and re-layouts: 122 us -> 18.9 us
  loops' own time: 7.16 us -> 0 us
    reduce_sum x36 -> x0, other arithmetic: 351 us -> none  [partial_sums(): sum_x = jnp.sum(pressure_term * gap_x, axis=(1, 3))]
    pallas_call x0 -> x1, Pallas kernels: none -> 232 us  [per_device(): pl.pallas_call(body, out_shape=jax.ShapeDtypeStruct((blocks, 4, slots), j...]
    gather x36 -> x0, local copies, waits for them, and re-layouts: 97.3 us -> none  [add_sources(): sources = lookup[code_part]]
    dynamic_slice x24 -> x0, local copies, waits for them, and re-layouts: 8.77 us -> none  [per_device(): output = lax.map(per_group, (group_targets, group_live, group_codes))]
    another operation x13 -> x0, loops' own time: 7.16 us -> none  [the longest x12 6.28 us: per_group(): total, unused = lax.scan(add_sources, start, split_codes)]
  transfers between devices with their start and end apart: 5 -> 5, of which waited for: 5 -> 2; matrix products, arithmetic and copies ran while one was open for 0% -> 3% of each run, Pallas kernels for 0% -> 0%
where the time goes in v1:
time: 333 us; the launch traced here: 332 us
  Pallas kernels  232 us (70%)
  waiting for transfers between devices  37 us (11%)
  other arithmetic  24.2 us (7%)
  local copies, waits for them, and re-layouts  18.9 us (6%)
  between operations  13.5 us (4%)
  starting transfers between devices  6.53 us (2%)
    pallas_call x1, Pallas kernels, per_device(): pl.pallas_call(body, out_shape=jax.ShapeDtypeStruct((blocks, 4, slots), j...  232 us
    all_gather x1, waiting for transfers between devices, per_device(): stacked = lax.all_gather(stacked, 'cross', axis=1, tiled=True)  27.2 us
    ppermute x4, waiting for transfers between devices, passed_along(): return lax.ppermute(value, axis, pairs)  9.71 us
    unnamed x15, local copies, waits for them, and re-layouts  6.78 us
  transfers between devices with their start and end apart: 5, of which 2 were waited for; matrix products, arithmetic and copies ran while one was open for 3% of the time, Pallas kernels for 0%

profile of v1, /device:TPU:2, one launch (start us, length us, event | category | flops | bytes accessed | tf_op | source)
XLA Modules:
  0.0 332.1 jit_solution(14128415510110617369)
XLA Ops:
  6.5 0.0 copy-start.1
  6.5 0.0 all-gather.2.cloned.1.call-start
  6.5 1.1 slice_add_fusion
  7.7 2.2 copy.47
  9.9 0.0 copy-done.1
  9.9 1.1 copy.58
  11.0 0.0 copy-start.3
  11.0 0.0 copy-start.2
  11.0 2.7 copy.49
  13.6 2.2 copy.48
  15.9 0.0 copy-done.2
  15.9 6.3 %fusion.4 = (f32[48,128]{1,0:T(8,128)}, f32[48,1,128]{1,2,0:T(8,128)S(1)}, f32[48,128]{1,0:T(8,128)}, f32[48,1,128]{1,2,0:T(8,128)S(1)}) fusion(f32[48,1,128]{1,2,0:T(8,128)} %copy.47, f32[48,1,128]{1,2,0:T(8,128)} %copy.48, f32[48,1,128]{1,2,0:T(8,128)} %copy.49, s32[48]{0:T(128)S(1)} %copy-done.2), kind=kLoop, calls=%fused_computation.18 | loop fusion | flops 24576 | bytes 172224 | tf_op jit(solution)/shard_map/mul | solution.py:140
  22.1 0.0 copy-start.4
  22.2 0.0 copy-start.5
  22.2 1.7 copy-done.4
  23.9 0.9 copy-done.5
  24.8 3.3 %pad_maximum_fusion = f32[48,8,128]{1,2,0:T(8,128)} fusion(f32[48,1,128]{1,2,0:T(8,128)S(1)} %get-tuple-element.13, f32[48,1,128]{1,2,0:T(8,128)S(1)} %get-tuple-element.8, f32[48,6,128]{1,2,0:T(8,128)S(1)} %copy.58), kind=kLoop, calls=%fused_computation | loop fusion | flops 98304 | bytes 393216 | tf_op jit(solution)/shard_map/concatenate | solution.py:142
  28.1 3.0 copy.50
  31.1 3.6 %collective-permute-start.3 = (f32[48,8,128]{2,1,0:T(8,128)}, f32[48,8,128]{2,1,0:T(8,128)}, u32[]{:S(2)}, u32[]{:S(2)}) collective-permute-start(f32[48,8,128]{2,1,0:T(8,128)} %copy.50), channel_id=1, source_target_pairs={{0,24},{4,28},{8,0},{12,4},{16,8},{20,12},{24,16},{28,20},{1,25},{... | collective-permute-start | bytes 589832 | tf_op jit(solution)/shard_map/ppermute | solution.py:29
  34.7 0.5 collective-permute-start.2
  35.2 2.4 collective-permute-start.1
  37.6 0.0 collective-permute-start
  37.6 0.0 copy-done.3
  37.6 1.2 copy.52
  38.8 9.7 %collective-permute-done = f32[48,8,128]{2,1,0:T(8,128)} collective-permute-done((f32[48,8,128]{2,1,0:T(8,128)}, f32[48,8,128]{2,1,0:T(8,128)}, u32[]{:S(2)}, u32[]{:S(2)}) %collective-permute-start) | collective-permute-done | bytes 196640 | tf_op jit(solution)/shard_map/ppermute | solution.py:29
  48.5 1.0 bitcast_dynamic-update-slice_fusion.3
  49.5 0.0 collective-permute-done.1
  49.6 1.0 bitcast_dynamic-update-slice_fusion.2
  50.6 0.8 maximum_dynamic-update-slice_fusion
  51.4 0.0 collective-permute-done.2
  51.4 1.0 bitcast_dynamic-update-slice_fusion.1
  52.4 0.0 collective-permute-done.3
  52.4 1.0 bitcast_dynamic-update-slice_fusion
  53.4 0.0 copy-start.6
  53.5 1.0 copy-done.6
  54.4 0.0 all-gather.2.cloned.1.call-update
  54.4 0.9 reshape.66.codes
  55.3 5.4 %fusion.6.columns = f32[48,128,8]{2,1,0:T(8,128)S(1)} fusion(f32[48,1,128]{1,2,0:T(8,128)} %copy-done.5, f32[48,1,128]{1,2,0:T(8,128)} %copy-done.4, f32[48,6,128]{1,2,0:T(8,128)} %copy-done.3), kind=kLoop, calls=%fused_computation.20 | loop fusion | flops 98304 | bytes 393216 | tf_op jit(solution)/shard_map/transpose | solution.py:151
  60.7 27.2 %all-gather.2.cloned.1.call-done = f32[5,192,8,128]{3,2,1,0:T(8,128)} async-done(((f32[5,48,8,128]{3,2,1,0:T(8,128)}), f32[5,192,8,128]{3,2,1,0:T(8,128)}) %all-gather.2.cloned.1.call-update) | async-done | bytes 3932176 | tf_op jit(solution)/shard_map/all_gather | solution.py:148
  88.0 2.9 slice_compare_fusion
  90.9 0.2 select_reduce_fusion.source_counts
  91.1 0.0 copy-start
  91.1 2.1 copy-done
  93.2 232.1 %pair_rates.1 = f32[48,4,128]{2,1,0:T(4,128)} custom-call(s32[2160]{0:T(1024)S(1)} %reshape.66.codes, s32[48]{0:T(128)S(1)} %copy-done.2, s32[960]{0:T(1024)S(1)} %select_reduce_fusion.source_counts, f32[48,8,128]{2,1,0:T(8,128)S(1)} %copy-done.1, f32[48,128,8]{2,1,0:T(8,128)S(1)} %fusion.6.columns, f32[960,8,128]{2,1,0:T(8,128)S(1)} %bitcast.23), custom_call_target="tpu_custom_call" | custom-call | tf_op jit(solution)/shard_map/pair_rates/pallas_call | solution.py:153
  (6 shorter events, 0.0 us)
Async XLA Ops:
  6.5 3.4 %copy-start.1 = (f32[48,8,128]{2,1,0:T(8,128)S(1)}, f32[48,8,128]{2,1,0:T(8,128)}, u32[]{:S(2)}) copy-start(f32[48,8,128]{2,1,0:T(8,128)} %target.1) | copy-start | bytes 589828
  6.5 81.4 %all-gather.2.cloned.1.call-start = ((), (), s32[]{:S(2)}) async-start(), calls=%async_computation | async-start | bytes 4915200 | tf_op jit(solution)/shard_map/all_gather | solution.py:148
  11.0 26.7 %copy-start.3 = (f32[48,6,128]{1,2,0:T(8,128)}, f32[48,6,128]{1,2,0:T(8,128)S(1)}, u32[]{:S(2)}) copy-start(f32[48,6,128]{1,2,0:T(8,128)S(1)} %copy.58) | copy-start | bytes 442372
  11.0 4.9 %copy-start.2 = (s32[48]{0:T(128)S(1)}, s32[48]{0:T(128)}, u32[]{:S(2)}) copy-start(s32[48]{0:T(128)} %live_counts.1) | copy-start | bytes 580
  22.1 1.8 copy-start.4
  22.2 2.6 copy-start.5
  31.1 21.3 %collective-permute-start.3 = (f32[48,8,128]{2,1,0:T(8,128)}, f32[48,8,128]{2,1,0:T(8,128)}, u32[]{:S(2)}, u32[]{:S(2)}) collective-permute-start(f32[48,8,128]{2,1,0:T(8,128)} %copy.50), channel_id=1, source_target_pairs={{0,24},{4,28},{8,0},{12,4},{16,8},{20,12},{24,16},{28,20},{1,25},{... | collective-permute-start | bytes 589832 | tf_op jit(solution)/shard_map/ppermute | solution.py:29
  34.7 16.7 %collective-permute-start.2 = (f32[48,8,128]{2,1,0:T(8,128)}, f32[48,8,128]{2,1,0:T(8,128)}, u32[]{:S(2)}, u32[]{:S(2)}) collective-permute-start(f32[48,8,128]{2,1,0:T(8,128)} %copy.50), channel_id=1, source_target_pairs={{0,28},{4,0},{8,4},{12,8},{16,12},{20,16},{24,20},{28,24},{1,29},{... | collective-permute-start | bytes 589832 | tf_op jit(solution)/shard_map/ppermute | solution.py:29
  35.2 14.3 %collective-permute-start.1 = (f32[48,8,128]{2,1,0:T(8,128)}, f32[48,8,128]{2,1,0:T(8,128)}, u32[]{:S(2)}, u32[]{:S(2)}) collective-permute-start(f32[48,8,128]{2,1,0:T(8,128)} %copy.50), channel_id=1, source_target_pairs={{0,4},{4,8},{8,12},{12,16},{16,20},{20,24},{24,28},{28,0},{1,5},{5... | collective-permute-start | bytes 589832 | tf_op jit(solution)/shard_map/ppermute | solution.py:29
  37.6 10.9 %collective-permute-start = (f32[48,8,128]{2,1,0:T(8,128)}, f32[48,8,128]{2,1,0:T(8,128)}, u32[]{:S(2)}, u32[]{:S(2)}) collective-permute-start(f32[48,8,128]{2,1,0:T(8,128)} %copy.50), channel_id=1, source_target_pairs={{0,8},{4,12},{8,16},{12,20},{16,24},{20,28},{24,0},{28,4},{1,9},{5... | collective-permute-start | bytes 589832 | tf_op jit(solution)/shard_map/ppermute | solution.py:29
  53.4 1.0 copy-start.6
  91.1 2.1 copy-start
Sparse Core Ops, SparseCore 0:
  54.6 33.3 all-gather.1

commit v2 on v0

v2 whole, which is shorter than its diff:
```python
import functools
import math

import jax
import jax.numpy as jnp
from jax import lax
from jax.experimental import pallas as pl
from jax.experimental.pallas import tpu as pltpu
from jax.sharding import PartitionSpec as P

GY = 8


kernel_coef = 5.0 * 21.0 / (16.0 * math.pi)
eta_square = 0.01
sound_speed = 6.0
delta_coef = 0.1
visc_coef = 0.1
slab_order = (-2, -1, 0, 1, 2)
wave = sound_speed * visc_coef
stiff = sound_speed / visc_coef
rows_step = 16
tiles_step = 4
fields = 7


def passed_along(value, axis, steps):
    count = lax.axis_size(axis)
    pairs = [(source, (source + steps) % count) for source in range(count)]
    return lax.ppermute(value, axis, pairs)


def ready_kernel(counts, particles, out):
    blocks, width, slots = particles.shape
    lanes = lax.broadcasted_iota(jnp.int32, (1, slots), 1)

    def one(block, unused):
        rho = particles[block, 6:7, :]
        out[block, 0:6, :] = particles[block, 0:6, :]
        out[block, 6:7, :] = stiff * (rho - 1.0)
        out[block, 7:8, :] = jnp.where(lanes < counts[block], particles[block, 7:8, :] / rho, 0.0)
        return unused

    lax.fori_loop(0, blocks, one, 0, unroll=8)


def pair_kernel(per_block, slab_blk, wide_y, wide_z, codes, live_counts, source_counts, particles, ready, lookup, out, packed, spread, totals):
    blocks, width, slots = particles.shape
    lanes = lax.broadcasted_iota(jnp.int32, (8, slots), 1)
    row = lax.broadcasted_iota(jnp.int32, (8, slots), 0)
    wide = jnp.where(row == 1, wide_y, jnp.where(row == 2, wide_z, 0.0))
    inverse = jnp.where(row == 1, 1.0 / wide_y, jnp.where(row == 2, 1.0 / wide_z, 0.0))
    along = jnp.where(row == 0, 1.0, 0.0)
    empty = jnp.zeros((8, slots), jnp.float32)
    scale = kernel_coef / 8.0

    def finish(block):
        rows = []
        for which in range(5):
            total = empty
            for group in range(slots // 8):
                part = jnp.sum(totals[which, group * 8:group * 8 + 8, :], axis=1, keepdims=True)
                total = total + jnp.where(lanes == row + group * 8, part, 0.0)
            rows.append(jnp.sum(total, axis=0, keepdims=True))
        rho = particles[block, 6:7, :]
        drho = scale * (2.0 * delta_coef * sound_speed / stiff * rows[1] - rho * rows[0])
        over = (scale * wave) / rho
        alive = lanes[0:1] < live_counts[block]
        out[block, 0:1, :] = jnp.where(alive, drho, 0.0)
        for axis in range(3):
            out[block, axis + 1:axis + 2, :] = jnp.where(alive, over * rows[2 + axis], 0.0)

    def per_block_step(block, unused):
        finish(jnp.maximum(block - 1, 0))
        own = ready[block]
        own_first = jnp.broadcast_to(own[:, 0:1], (8, slots)) * inverse + 0.5

        current, tile, start = empty, jnp.int32(0), jnp.int32(0)
        for step in range(per_block):
            code = codes[block * per_block + step]
            count = source_counts[code]
            slab = jnp.int32(-2)
            for border in range(1, 5):
                slab = slab + (code >= border * slab_blk).astype(jnp.int32)
            value = lookup[code]
            first = jnp.broadcast_to(value[:, 0:1], (8, slots))
            value = value + (wide * jnp.floor(own_first - first * inverse) + along * slab.astype(jnp.float32))
            turned = pltpu.roll(value, start, 1)
            ahead = lanes >= start
            merged = jnp.where(ahead, turned, current)
            packed[tile] = merged
            end = start + count
            full = (end >= slots).astype(jnp.int32)
            keep = jnp.broadcast_to(full, (8, slots)) == 0
            rest = jnp.where(ahead, 0.0, turned)
            current = jnp.where(keep, merged, rest)
            tile = tile + full
            start = end - full * slots
        packed[tile] = current
        for more in range(1, tiles_step):
            packed[tile + more] = empty
        tiles = tile + (start > 0).astype(jnp.int32)

        columns = jnp.transpose(own)
        for group in range(slots // 8):
            for field in range(fields):
                spread[field, group * 8:group * 8 + 8, :] = jnp.broadcast_to(
                    columns[group * 8:group * 8 + 8, field:field + 1], (8, slots)
                )

        live = live_counts[block]

        def per_rows(index, unused):
            first = pl.multiple_of(index * rows_step, rows_step)
            rows = pl.ds(first, rows_step)
            xi, yi, zi, ui, vi, wi, pi = [spread[field, rows, :] for field in range(fields)]

            def one_tile(place, sums):
                s_close, s_diff, s_damp, s_x, s_y, s_z = sums
                xj, yj, zj, uj, vj, wj, pj, volume = [packed[place, field:field + 1, :] for field in range(8)]
                gap_x = xi - xj
                gap_y = yi - yj
                gap_z = zi - zj
                shifted = (gap_x * gap_x + eta_square) + (gap_y * gap_y + gap_z * gap_z)
                inv = lax.rsqrt(shifted)
                bump = jnp.maximum(2.0 - shifted * inv, 0.0)
                weight = (bump * bump) * (bump * volume)
                closing = (ui - uj) * gap_x + (vi - vj) * gap_y + (wi - wj) * gap_z
                inv_sq = inv * inv
                diff = weight * (pj - pi)
                push = weight * ((pi + pj) - closing * inv_sq)
                return (
                    s_close + weight * closing,
                    s_diff + diff,
                    s_damp + diff * inv_sq,
                    s_x + push * gap_x,
                    s_y + push * gap_y,
                    s_z + push * gap_z,
                )

            def some_tiles(place, sums):
                for more in range(tiles_step):
                    sums = one_tile(tiles_step * place + more, sums)
                return sums

            zero = jnp.zeros((rows_step, slots), jnp.float32)
            sums = lax.fori_loop(0, (tiles + tiles_step - 1) // tiles_step, some_tiles, (zero,) * 6)
            totals[0, rows, :] = sums[0]
            totals[1, rows, :] = sums[1] - eta_square * sums[2]
            totals[2, rows, :] = sums[3]
            totals[3, rows, :] = sums[4]
            totals[4, rows, :] = sums[5]
            return unused

        lax.fori_loop(0, (live + rows_step - 1) // rows_step, per_rows, 0)
        return unused

    lax.fori_loop(0, blocks, per_block_step, 0)
    finish(blocks - 1)


def per_device(particles, counts, pairs):
    blocks, width, slots = particles.shape
    slab_blk = blocks * lax.axis_size("cross")
    cells_z = slab_blk // GY
    per_block = pairs.shape[1]
    vmem = pl.BlockSpec(memory_space=pltpu.VMEM)
    smem = pl.BlockSpec(memory_space=pltpu.SMEM)
    limit = pltpu.CompilerParams(vmem_limit_bytes=40 * 1024 * 1024)
    ready = pl.pallas_call(
        ready_kernel,
        out_shape=jax.ShapeDtypeStruct(particles.shape, jnp.float32),
        in_specs=[smem, vmem],
        out_specs=vmem,
        compiler_params=limit,
        name="ready",
    )(counts, particles)
    nearby = {0: ready}
    for offset in (1, -1, 2, -2):
        nearby[offset] = passed_along(ready, "flow", -offset)
    stacked = jnp.stack([nearby[offset] for offset in slab_order])
    stacked = lax.all_gather(stacked, "cross", axis=1, tiled=True)
    lookup = stacked.reshape((5 * slab_blk, width, slots))
    slot_ids = jnp.arange(slots, dtype=jnp.int32)
    source_counts = jnp.max(jnp.where(lookup[:, 7] > 0.0, slot_ids[None, :] + 1, 0), axis=1)
    body = functools.partial(pair_kernel, per_block, slab_blk, 2.0 * GY, 2.0 * cells_z)
    return pl.pallas_call(
        body,
        out_shape=jax.ShapeDtypeStruct((blocks, 4, slots), jnp.float32),
        in_specs=[smem, smem, smem, vmem, vmem, vmem],
        out_specs=vmem,
        scratch_shapes=[
            pltpu.VMEM((per_block + tiles_step + 1, 8, slots), jnp.float32),
            pltpu.VMEM((fields, slots, slots), jnp.float32),
            pltpu.VMEM((5, slots, slots), jnp.float32),
        ],
        compiler_params=limit,
        name="pair_rates",
    )(pairs.reshape(-1), counts, source_counts, particles, ready, lookup)


def solution(mesh):
    placed = (P(("flow", "cross"), None, None), P(("flow", "cross")), P(("flow", "cross"), None))
    return jax.shard_map(
        per_device,
        mesh=mesh,
        in_specs=placed,
        out_specs=P(("flow", "cross"), None, None),
        check_vma=False,
    )
```

time: 552 us -> 230 us (0.42)
  the two profiles are of different devices: /device:TPU:2 before, /device:TPU:27 now
where the time goes in v2:
time: 230 us; the launch traced here: 229 us
  Pallas kernels  158 us (69%)
  waiting for transfers between devices  45.9 us (20%)
  between operations  13.5 us (6%)
  local copies, waits for them, and re-layouts  5.56 us (2%)
  other arithmetic  3.09 us (1%)
  starting transfers between devices  2.98 us (1%)
    pallas_call x1, Pallas kernels, per_device(): pl.pallas_call(body, out_shape=jax.ShapeDtypeStruct((blocks, 4, slots), j...  157 us
    all_gather x1, waiting for transfers between devices, per_device(): stacked = lax.all_gather(stacked, 'cross', axis=1, tiled=True)  34.8 us
    ppermute x4, waiting for transfers between devices, passed_along(): return lax.ppermute(value, axis, pairs)  11 us
    unnamed x16, local copies, waits for them, and re-layouts  4.69 us
  transfers between devices with their start and end apart: 5, of which 5 were waited for; matrix products, arithmetic and copies ran while one was open for 0% of the time, Pallas kernels for 0%

profile of v2, /device:TPU:27, one launch (start us, length us, event | category | flops | bytes accessed | tf_op | source)
XLA Modules:
  0.0 229.0 jit_solution(5799267388034820877)
XLA Ops:
  6.5 0.0 all-gather.2.cloned.1.call-start
  6.5 0.0 copy-start.1
  6.5 0.9 copy-done.1
  7.5 0.0 copy-start.3
  7.5 0.7 copy-done.3
  8.1 0.0 copy-start.2
  8.1 0.0 copy-start.4
  8.1 0.6 ready.1
  8.8 0.1 collective-permute-start
  8.8 1.2 collective-permute-start.1
  10.0 0.3 collective-permute-start.2
  10.4 1.4 collective-permute-start.3
  11.8 2.8 %collective-permute-done = f32[48,8,128]{2,1,0:T(8,128)S(1)} collective-permute-done((f32[48,8,128]{2,1,0:T(8,128)S(1)}, f32[48,8,128]{2,1,0:T(8,128)S(1)}, u32[]{:S(2)}, u32[]{:S(2)}) %collective-permute-start) | collective-permute-done | bytes 196640 | tf_op jit(solution)/shard_map/ppermute | solution.py:30
  14.6 2.1 collective-permute-done.1
  16.8 1.3 collective-permute-done.2
  18.1 4.8 %collective-permute-done.3 = f32[48,8,128]{2,1,0:T(8,128)S(1)} collective-permute-done((f32[48,8,128]{2,1,0:T(8,128)S(1)}, f32[48,8,128]{2,1,0:T(8,128)S(1)}, u32[]{:S(2)}, u32[]{:S(2)}) %collective-permute-start.3) | collective-permute-done | bytes 196640 | tf_op jit(solution)/shard_map/ppermute | solution.py:30
  22.9 0.0 copy-start.5
  22.9 0.9 copy-done.5
  23.9 0.0 all-gather.2.cloned.1.call-update
  23.9 0.9 reshape.13.codes
  24.7 34.8 %all-gather.2.cloned.1.call-done = f32[5,192,8,128]{3,2,1,0:T(8,128)} async-done(((f32[5,48,8,128]{3,2,1,0:T(8,128)}), f32[5,192,8,128]{3,2,1,0:T(8,128)}) %all-gather.2.cloned.1.call-update) | async-done | bytes 3932176 | tf_op jit(solution)/shard_map/all_gather | solution.py:182
  59.5 2.9 %slice_compare_fusion = pred[960,1,128]{2,1,0:T(4,128)(4,1)S(1)} fusion(f32[960,8,128]{2,1,0:T(8,128)} %bitcast.13), kind=kLoop, calls=%fused_computation | loop fusion | flops 122880 | bytes 614400 | tf_op jit(solution)/shard_map/gt | solution.py:185
  62.4 0.2 select_reduce_fusion.source_counts
  62.6 0.0 copy-done.2
  62.6 0.0 copy-done.4
  62.7 0.0 copy-start
  62.7 2.1 copy-done
  64.8 157.4 %pair_rates.1 = f32[48,4,128]{2,1,0:T(4,128)} custom-call(s32[2160]{0:T(1024)S(1)} %reshape.13.codes, s32[48]{0:T(128)S(1)} %copy-done.4, s32[960]{0:T(1024)S(1)} %select_reduce_fusion.source_counts, f32[48,8,128]{2,1,0:T(8,128)S(1)} %copy-done.2, f32[48,8,128]{2,1,0:T(8,128)S(1)} %ready.1, f32[960,8,128]{2,1,0:T(8,128)S(1)} %bitcast.14), custom_call_target="tpu_custom_call" | custom-call | tf_op jit(solution)/shard_map/pair_rates/pallas_call | solution.py:187
  (6 shorter events, 0.1 us)
Async XLA Ops:
  6.5 53.0 %all-gather.2.cloned.1.call-start = ((), (), s32[]{:S(2)}) async-start(), calls=%async_computation | async-start | bytes 4915200 | tf_op jit(solution)/shard_map/all_gather | solution.py:182
  6.5 0.9 copy-start.1
  7.5 0.7 copy-start.3
  8.1 54.5 %copy-start.2 = (f32[48,8,128]{2,1,0:T(8,128)S(1)}, f32[48,8,128]{2,1,0:T(8,128)}, u32[]{:S(2)}) copy-start(f32[48,8,128]{2,1,0:T(8,128)} %particles.3) | copy-start | bytes 589828
  8.1 54.5 %copy-start.4 = (s32[48]{0:T(128)S(1)}, s32[48]{0:T(128)}, u32[]{:S(2)}) copy-start(s32[48]{0:T(128)} %live_counts.1) | copy-start | bytes 580
  8.8 5.8 %collective-permute-start = (f32[48,8,128]{2,1,0:T(8,128)S(1)}, f32[48,8,128]{2,1,0:T(8,128)S(1)}, u32[]{:S(2)}, u32[]{:S(2)}) collective-permute-start(f32[48,8,128]{2,1,0:T(8,128)S(1)} %ready.1), channel_id=1, source_target_pairs={{0,8},{4,12},{8,16},{12,20},{16,24},{20,28},{24,0},{28,4},{1,9},{5... | collective-permute-start | bytes 589832 | tf_op jit(solution)/shard_map/ppermute | solution.py:30
  8.8 7.9 %collective-permute-start.1 = (f32[48,8,128]{2,1,0:T(8,128)S(1)}, f32[48,8,128]{2,1,0:T(8,128)S(1)}, u32[]{:S(2)}, u32[]{:S(2)}) collective-permute-start(f32[48,8,128]{2,1,0:T(8,128)S(1)} %ready.1), channel_id=1, source_target_pairs={{0,4},{4,8},{8,12},{12,16},{16,20},{20,24},{24,28},{28,0},{1,5},{5... | collective-permute-start | bytes 589832 | tf_op jit(solution)/shard_map/ppermute | solution.py:30
  10.0 8.0 %collective-permute-start.2 = (f32[48,8,128]{2,1,0:T(8,128)S(1)}, f32[48,8,128]{2,1,0:T(8,128)S(1)}, u32[]{:S(2)}, u32[]{:S(2)}) collective-permute-start(f32[48,8,128]{2,1,0:T(8,128)S(1)} %ready.1), channel_id=1, source_target_pairs={{0,28},{4,0},{8,4},{12,8},{16,12},{20,16},{24,20},{28,24},{1,29},{... | collective-permute-start | bytes 589832 | tf_op jit(solution)/shard_map/ppermute | solution.py:30
  10.4 12.5 %collective-permute-start.3 = (f32[48,8,128]{2,1,0:T(8,128)S(1)}, f32[48,8,128]{2,1,0:T(8,128)S(1)}, u32[]{:S(2)}, u32[]{:S(2)}) collective-permute-start(f32[48,8,128]{2,1,0:T(8,128)S(1)} %ready.1), channel_id=1, source_target_pairs={{0,24},{4,28},{8,0},{12,4},{16,8},{20,12},{24,16},{28,20},{1,25},{... | collective-permute-start | bytes 589832 | tf_op jit(solution)/shard_map/ppermute | solution.py:30
  22.9 0.9 copy-start.5
  62.7 2.1 copy-start
Sparse Core Ops, SparseCore 0:
  24.0 35.5 all-gather.1

commit v3 on v2

--- a/solution.py
+++ b/solution.py
@@ -20,7 +20,7 @@
 wave = sound_speed * visc_coef
 stiff = sound_speed / visc_coef
 rows_step = 16
-tiles_step = 4
+tiles_steps = (8, 4)
 fields = 7
 
 
@@ -28,6 +28,14 @@
     count = lax.axis_size(axis)
     pairs = [(source, (source + steps) % count) for source in range(count)]
     return lax.ppermute(value, axis, pairs)
+
+
+def in_order(codes):
+    places = jnp.arange(codes.shape[1], dtype=jnp.int32)
+    mine, other = codes[:, :, None], codes[:, None, :]
+    before = (other < mine) | ((other == mine) & (places[None, None, :] < places[None, :, None]))
+    rank = jnp.sum(before.astype(jnp.int32), axis=2)
+    return jnp.sum(jnp.where(rank[:, None, :] == places[None, :, None], codes[:, None, :], 0), axis=2)
 
 
 def ready_kernel(counts, particles, out):
@@ -44,7 +52,10 @@
     lax.fori_loop(0, blocks, one, 0, unroll=8)
 
 
-def pair_kernel(per_block, slab_blk, wide_y, wide_z, codes, live_counts, source_counts, particles, ready, lookup, out, packed, spread, totals):
+def pair_kernel(slabs, wide_y, wide_z, codes, live_counts, source_counts, particles, ready, lookup, *rest_refs):
+    earlier = rest_refs[0] if len(rest_refs) == 5 else None
+    out, packed, spread, totals = rest_refs[-4:]
+    per_block = len(slabs)
     blocks, width, slots = particles.shape
     lanes = lax.broadcasted_iota(jnp.int32, (8, slots), 1)
     row = lax.broadcasted_iota(jnp.int32, (8, slots), 0)
@@ -66,9 +77,11 @@
         drho = scale * (2.0 * delta_coef * sound_speed / stiff * rows[1] - rho * rows[0])
         over = (scale * wave) / rho
         alive = lanes[0:1] < live_counts[block]
-        out[block, 0:1, :] = jnp.where(alive, drho, 0.0)
-        for axis in range(3):
-            out[block, axis + 1:axis + 2, :] = jnp.where(alive, over * rows[2 + axis], 0.0)
+        results = [drho] + [over * rows[2 + axis] for axis in range(3)]
+        for place, result in enumerate(results):
+            if earlier is not None:
+                result = result + earlier[block, place:place + 1, :]
+            out[block, place:place + 1, :] = jnp.where(alive, result, 0.0)
 
     def per_block_step(block, unused):
         finish(jnp.maximum(block - 1, 0))
@@ -79,12 +92,9 @@
         for step in range(per_block):
             code = codes[block * per_block + step]
             count = source_counts[code]
-            slab = jnp.int32(-2)
-            for border in range(1, 5):
-                slab = slab + (code >= border * slab_blk).astype(jnp.int32)
             value = lookup[code]
             first = jnp.broadcast_to(value[:, 0:1], (8, slots))
-            value = value + (wide * jnp.floor(own_first - first * inverse) + along * slab.astype(jnp.float32))
+            value = value + (wide * jnp.floor(own_first - first * inverse) + along * slabs[step])
             turned = pltpu.roll(value, start, 1)
             ahead = lanes >= start
             merged = jnp.where(ahead, turned, current)
@@ -97,7 +107,7 @@
             tile = tile + full
             start = end - full * slots
         packed[tile] = current
-        for more in range(1, tiles_step):
+        for more in range(1, tiles_steps[-1]):
             packed[tile + more] = empty
         tiles = tile + (start > 0).astype(jnp.int32)
 
@@ -138,13 +148,19 @@
                     s_z + push * gap_z,
                 )
 
-            def some_tiles(place, sums):
-                for more in range(tiles_step):
-                    sums = one_tile(tiles_step * place + more, sums)
-                return sums
-
-            zero = jnp.zeros((rows_step, slots), jnp.float32)
-            sums = lax.fori_loop(0, (tiles + tiles_step - 1) // tiles_step, some_tiles, (zero,) * 6)
+            sums = (jnp.zeros((rows_step, slots), jnp.float32),) * 6
+            begin = jnp.int32(0)
+            for step in tiles_steps:
+                last = step == tiles_steps[-1]
+                turns = (tiles - begin + (step - 1 if last else 0)) // step
+
+                def some_tiles(turn, sums, step=step, begin=begin):
+                    for more in range(step):
+                        sums = one_tile(begin + turn * step + more, sums)
+                    return sums
+
+                sums = lax.fori_loop(0, turns, some_tiles, sums)
+                begin = begin + turns * step
             totals[0, rows, :] = sums[0]
             totals[1, rows, :] = sums[1] - eta_square * sums[2]
             totals[2, rows, :] = sums[3]
@@ -175,28 +191,40 @@
         compiler_params=limit,
         name="ready",
     )(counts, particles)
-    nearby = {0: ready}
-    for offset in (1, -1, 2, -2):
-        nearby[offset] = passed_along(ready, "flow", -offset)
-    stacked = jnp.stack([nearby[offset] for offset in slab_order])
-    stacked = lax.all_gather(stacked, "cross", axis=1, tiled=True)
-    lookup = stacked.reshape((5 * slab_blk, width, slots))
-    slot_ids = jnp.arange(slots, dtype=jnp.int32)
-    source_counts = jnp.max(jnp.where(lookup[:, 7] > 0.0, slot_ids[None, :] + 1, 0), axis=1)
-    body = functools.partial(pair_kernel, per_block, slab_blk, 2.0 * GY, 2.0 * cells_z)
-    return pl.pallas_call(
-        body,
-        out_shape=jax.ShapeDtypeStruct((blocks, 4, slots), jnp.float32),
-        in_specs=[smem, smem, smem, vmem, vmem, vmem],
-        out_specs=vmem,
-        scratch_shapes=[
-            pltpu.VMEM((per_block + tiles_step + 1, 8, slots), jnp.float32),
-            pltpu.VMEM((fields, slots, slots), jnp.float32),
-            pltpu.VMEM((5, slots, slots), jnp.float32),
-        ],
-        compiler_params=limit,
-        name="pair_rates",
-    )(pairs.reshape(-1), counts, source_counts, particles, ready, lookup)
+    nearby = {offset: passed_along(ready, "flow", -offset) for offset in slab_order if offset}
+    listed = in_order(pairs)
+    per_slab = per_block // len(slab_order)
+    middle = per_slab * (len(slab_order) // 2)
+    own_codes = listed[:, middle:middle + per_slab] - 2 * slab_blk
+    far_codes = jnp.concatenate([listed[:, :middle], listed[:, middle + per_slab:] - slab_blk], axis=1)
+    own_lookup = lax.all_gather(ready, "cross", axis=0, tiled=True)
+    stacked = jnp.stack([nearby[offset] for offset in slab_order if offset])
+    stacked, own_lookup = lax.optimization_barrier((stacked, own_lookup))
+    far_lookup = lax.all_gather(stacked, "cross", axis=1, tiled=True)
+    far_lookup = far_lookup.reshape((4 * slab_blk, width, slots))
+
+    def rates(slabs, codes, lookup, earlier, name):
+        slot_ids = jnp.arange(slots, dtype=jnp.int32)
+        source_counts = jnp.max(jnp.where(lookup[:, 7] > 0.0, slot_ids[None, :] + 1, 0), axis=1)
+        work = blocks * slots * slots * len(slabs)
+        return pl.pallas_call(
+            functools.partial(pair_kernel, slabs, 2.0 * GY, 2.0 * cells_z),
+            out_shape=jax.ShapeDtypeStruct((blocks, 4, slots), jnp.float32),
+            in_specs=[smem, smem, smem, vmem, vmem, vmem] + [vmem] * len(earlier),
+            out_specs=vmem,
+            scratch_shapes=[
+                pltpu.VMEM((len(slabs) + max(tiles_steps) + 1, 8, slots), jnp.float32),
+                pltpu.VMEM((fields, slots, slots), jnp.float32),
+                pltpu.VMEM((5, slots, slots), jnp.float32),
+            ],
+            compiler_params=limit,
+            cost_estimate=pl.CostEstimate(flops=60 * work, bytes_accessed=4 * lookup.size, transcendentals=work),
+            name=name,
+        )(codes.reshape(-1), counts, source_counts, particles, ready, lookup, *earlier)
+
+    own_rates = rates((0.0,) * per_slab, own_codes, own_lookup, (), "own_slab")
+    far_slabs = tuple(float(offset) for offset in slab_order if offset for _ in range(per_slab))
+    return rates(far_slabs, far_codes, far_lookup, (own_rates,), "other_slabs")
 
 
 def solution(mesh):

time: 230 us -> 241 us (1.048)
  the two profiles are of different devices: /device:TPU:27 before, /device:TPU:3 now
where the time goes in v3:
time: 241 us; the launch traced here: 237 us
  Pallas kernels  198 us (82%)
  between operations  13.5 us (6%)
  blocking collectives  10.1 us (4%)
  starting transfers between devices  4.91 us (2%)
  other arithmetic  4.52 us (2%)
  local copies, waits for them, and re-layouts  4.11 us (2%)
    pallas_call x2, Pallas kernels, rates(): pl.pallas_call(functools.partial(pair_kernel, slabs, 2.0 * GY, 2.0 * cell...  197 us
    all_gather x1, blocking collectives, per_device(): own_lookup = lax.all_gather(ready, 'cross', axis=0, tiled=True)  10.1 us
    ppermute x4, starting transfers between devices, passed_along(): return lax.ppermute(value, axis, pairs)  4.91 us
  transfers between devices with their start and end apart: 5, of which 1 were waited for; matrix products, arithmetic and copies ran while one was open for 1% of the time, Pallas kernels for 29%

profile of v3, /device:TPU:3, one launch (start us, length us, event | category | flops | bytes accessed | tf_op | source)
XLA Modules:
  0.0 237.2 jit_solution(6707040237976555119)
XLA Ops:
  6.5 0.0 all-gather.2.cloned.1.call-start
  6.5 0.0 copy-start
  6.5 0.9 copy-done
  7.5 0.0 copy-start.3
  7.5 0.7 copy-done.3
  8.1 0.6 ready.1
  8.8 1.3 collective-permute-start
  10.1 1.3 collective-permute-start.1
  11.4 0.2 collective-permute-start.2
  11.6 2.1 collective-permute-start.3
  13.7 10.1 %all_gather.6.lookup = f32[192,8,128]{2,1,0:T(8,128)S(1)} all-gather(f32[48,8,128]{2,1,0:T(8,128)S(1)} %ready.1), channel_id=1, replica_groups=mesh['flow'=8,'cross'=4] {'cross'}, dimensions={0}, use_global_device_ids=true | all-gather | bytes 983040 | tf_op jit(solution)/shard_map/all_gather | solution.py:200
  23.8 0.0 collective-permute-done
  23.8 0.0 collective-permute-done.1
  23.8 0.0 collective-permute-done.2
  23.8 2.1 collective-permute-done.3
  25.9 0.0 copy-start.5
  25.9 0.9 pad_maximum_fusion
  26.8 0.0 all-gather.2.cloned.1.call-update
  26.8 0.0 copy-done.5
  26.9 0.0 copy-start.1
  26.9 0.0 copy-start.4
  26.9 0.1 copy.5
  27.0 0.6 convert_reduce_fusion
  27.6 0.2 select_reduce_fusion
  27.8 0.1 copy.8
  27.9 0.1 reshape.38.codes
  28.0 0.1 copy.7
  28.1 0.1 reshape.36.codes
  28.2 0.2 copy.9
  28.4 0.1 select_reduce_fusion.2.source_counts
  28.5 0.0 copy-done.1
  28.5 0.0 copy-done.4
  28.5 68.8 %own_slab.1.rest_refs_0_ = f32[48,4,128]{2,1,0:T(4,128)S(1)} custom-call(s32[432]{0:T(512)S(1)} %reshape.38.codes, s32[48]{0:T(128)S(1)} %copy-done.4, s32[192]{0:T(256)S(1)} %select_reduce_fusion.2.source_counts, f32[48,8,128]{2,1,0:T(8,128)S(1)} %copy-done.1, f32[48,8,128]{2,1,0:T(8,128)S(1)} %ready.1, f32[192,8,128]{2,1,0:T(8,128)S(1)} %all_gather.6.lookup), custom_call_target="tpu_custom_call" | custom-call | flops 424673280 | bytes 786432 | tf_op jit(solution)/shard_map/own_slab/pallas_call | solution.py:210
  97.4 0.0 all-gather.2.cloned.1.call-done
  97.4 2.5 %slice_compare_fusion = pred[768,1,128]{2,1,0:T(4,128)(4,1)S(1)} fusion(f32[768,8,128]{2,1,0:T(8,128)} %bitcast.11), kind=kLoop, calls=%fused_computation.4 | loop fusion | flops 98304 | bytes 491520 | tf_op jit(solution)/shard_map/gt | solution.py:208
  99.9 0.2 select_reduce_fusion.1.source_counts
  100.1 0.0 copy-start.2
  100.1 1.9 copy-done.2
  102.0 128.4 %other_slabs.1 = f32[48,4,128]{2,1,0:T(4,128)} custom-call(s32[1728]{0:T(1024)S(1)} %reshape.36.codes, s32[48]{0:T(128)S(1)} %copy-done.4, s32[768]{0:T(1024)S(1)} %select_reduce_fusion.1.source_counts, f32[48,8,128]{2,1,0:T(8,128)S(1)} %copy-done.1, f32[48,8,128]{2,1,0:T(8,128)S(1)} %ready.1, f32[768,8,128]{2,1,0:T(8,128)S(1)} %bitcast.12, ...), custom_call_target="tpu_custom_call" | custom-call | flops 1698693120 | bytes 3145728 | tf_op jit(solution)/shard_map/other_slabs/pallas_call | solution.py:210
  (5 shorter events, 0.0 us)
Async XLA Ops:
  6.5 90.8 %all-gather.2.cloned.1.call-start = ((), (), s32[]{:S(2)}) async-start(), calls=%async_computation | async-start | bytes 3932160 | tf_op jit(solution)/shard_map/all_gather | solution.py:203
  6.5 0.9 copy-start
  7.5 0.7 copy-start.3
  8.8 15.0 %collective-permute-start = (f32[48,8,128]{2,1,0:T(8,128)S(1)}, f32[48,8,128]{2,1,0:T(8,128)S(1)}, u32[]{:S(2)}, u32[]{:S(2)}) collective-permute-start(f32[48,8,128]{2,1,0:T(8,128)S(1)} %ready.1), channel_id=1, source_target_pairs={{0,8},{4,12},{8,16},{12,20},{16,24},{20,28},{24,0},{28,4},{1,9},{5... | collective-permute-start | bytes 589832 | tf_op jit(solution)/shard_map/ppermute | solution.py:30
  10.1 13.7 %collective-permute-start.1 = (f32[48,8,128]{2,1,0:T(8,128)S(1)}, f32[48,8,128]{2,1,0:T(8,128)S(1)}, u32[]{:S(2)}, u32[]{:S(2)}) collective-permute-start(f32[48,8,128]{2,1,0:T(8,128)S(1)} %ready.1), channel_id=1, source_target_pairs={{0,4},{4,8},{8,12},{12,16},{16,20},{20,24},{24,28},{28,0},{1,5},{5... | collective-permute-start | bytes 589832 | tf_op jit(solution)/shard_map/ppermute | solution.py:30
  11.4 12.4 %collective-permute-start.2 = (f32[48,8,128]{2,1,0:T(8,128)S(1)}, f32[48,8,128]{2,1,0:T(8,128)S(1)}, u32[]{:S(2)}, u32[]{:S(2)}) collective-permute-start(f32[48,8,128]{2,1,0:T(8,128)S(1)} %ready.1), channel_id=1, source_target_pairs={{0,28},{4,0},{8,4},{12,8},{16,12},{20,16},{24,20},{28,24},{1,29},{... | collective-permute-start | bytes 589832 | tf_op jit(solution)/shard_map/ppermute | solution.py:30
  11.6 14.3 %collective-permute-start.3 = (f32[48,8,128]{2,1,0:T(8,128)S(1)}, f32[48,8,128]{2,1,0:T(8,128)S(1)}, u32[]{:S(2)}, u32[]{:S(2)}) collective-permute-start(f32[48,8,128]{2,1,0:T(8,128)S(1)} %ready.1), channel_id=1, source_target_pairs={{0,24},{4,28},{8,0},{12,4},{16,8},{20,12},{24,16},{28,20},{1,25},{... | collective-permute-start | bytes 589832 | tf_op jit(solution)/shard_map/ppermute | solution.py:30
  25.9 1.0 copy-start.5
  26.9 1.7 copy-start.1
  26.9 1.6 copy-start.4
  100.1 1.9 copy-start.2
Sparse Core Ops, SparseCore 0:
  27.0 28.2 all-gather.1
